TPU v7x, 32 devices: a whole 2x2x4 slice. The times are simulated.
32 devices in a mesh: gx: 8 (over z, core), gy: 4 (over y, x).
Axes of the slice: x: 2, y: 2, z: 4, core: 2. Of those that a mesh axis runs over, the one named last changes fastest.
Arguments:
- wave_tokens: bfloat16 [64, 128, 512], P('gx', 'gy'), may hold values from -6 to 6
- grad_out: bfloat16 [64, 128, 512], P('gx', 'gy'), may hold values from -6 to 6
- w_qkv: bfloat16 [512, 1536], replicated, may hold values from -0.25 to 0.25
- w_proj: bfloat16 [512, 512], replicated, may hold values from -0.25 to 0.25
- w_fc1: bfloat16 [512, 2048], replicated, may hold values from -0.25 to 0.25
- w_fc2: bfloat16 [2048, 512], replicated, may hold values from -0.125 to 0.125
- gain_attn: float32 [512], replicated, may hold values from 0.25 to 1.75
- gain_mlp: float32 [512], replicated, may hold values from 0.25 to 1.75
- attn_scale: float32 [16], replicated, may hold values from 2 to 16
- bias_table: float32 [16, 225], replicated, may hold values from -4 to 4
- r_wq: bfloat16 [512, 512], replicated, may hold values from -0.25 to 0.25
- r_wkv: bfloat16 [512, 1024], replicated, may hold values from -0.25 to 0.25
- r_wo: bfloat16 [512, 512], replicated, may hold values from -0.25 to 0.25
- read_scale: float32 [16], replicated, may hold values from 2 to 16
- floe_feat: bfloat16 [32, 768, 512], P(('gx', 'gy')), may hold values from -6 to 6
- floe_count: int32 [32], P(('gx', 'gy')), may hold values from 1 to 768, 8192 in all
- floe_patch: int32 [32, 768], P(('gx', 'gy')), may hold values from 0 to 8191, as said below
- floe_cover: int32 [32, 3, 768], P(('gx', 'gy')), may hold values 0 or 1
Outputs:
- patch_out: bfloat16 [64, 128, 512], P('gx', 'gy')
- grad_in: bfloat16 [64, 128, 512], P('gx', 'gy')
- floe_out: bfloat16 [32, 768, 512], P(('gx', 'gy'))
Inputs may be any that keep to these rules, and one draw needn't show every extreme that they name: `floe_patch`: among one device's 768 slots, exactly 24 name a patch in each device's block of 8 x 32 patches. The live floes of a device are its first floe_count slots; the counts sum to 8192 and the largest is 768.
All inputs are finite; a program needn't handle non-finite values. No bound on the sum of `floe_cover` on one device may be relied on, other than what follows from the above.
Results may differ from a plain program's by a relative error of at most 0.02.
Values may be sent and summed in bfloat16 or wider, within the bound.
A program may use at most 128 MiB of HBM per device.

v0:
```python
import jax
import jax.numpy as jnp
import numpy as np
from jax import lax
from jax.experimental import pallas as pl
from jax.experimental.pallas import tpu as pltpu
from jax.sharding import PartitionSpec as P

WIN = 8
SHIFT = 4
SPAN = WIN * WIN
LANES = 128
F32 = jnp.float32
BF16 = jnp.bfloat16
GELU_A = 0.7978845608028654
GELU_B = 0.044715
NN = (((1,), (0,)), ((), ()))
NT = (((1,), (1,)), ((), ()))
TN = (((0,), (0,)), ((), ()))


def dot(a, b, dims=NN):
    return lax.dot_general(a, b, dims, preferred_element_type=F32)


def split_dot(values, ones):
    high = values.astype(BF16)
    low = (values - high.astype(F32)).astype(BF16)
    return dot(jnp.concatenate([high, low], 1), ones)


def block_ones(rows, cols, row_size, col_size):
    r = lax.broadcasted_iota(jnp.int32, (rows, cols), 0) // row_size
    c = lax.broadcasted_iota(jnp.int32, (rows, cols), 1) // col_size
    return jnp.where(r == c, 1.0, 0.0).astype(BF16)


def to_windows(block):
    rows, cols, width = block.shape
    parts = [block[:, w * WIN : (w + 1) * WIN, :].reshape(SPAN, width) for w in range(cols // WIN)]
    return jnp.concatenate(parts, 0)


def from_windows(flat):
    count = flat.shape[0] // SPAN
    parts = [flat[w * SPAN : (w + 1) * SPAN].reshape(WIN, WIN, flat.shape[1]) for w in range(count)]
    return jnp.concatenate(parts, 1)


def norm_parts(values):
    mean = jnp.mean(values, -1, keepdims=True)
    centred = values - mean
    inv = lax.rsqrt(jnp.mean(centred * centred, -1, keepdims=True) + 1e-05)
    return centred * inv, inv


def norm_back(cot, unit, inv):
    return inv * (
        cot - jnp.mean(cot, -1, keepdims=True) - unit * jnp.mean(cot * unit, -1, keepdims=True)
    )


def forward_kernel(
    x_ref, w_qkv, w_proj, w_fc1, w_fc2, gain_attn, gain_mlp, scale_ref, bias_ref,
    out_ref, qs_ref, kn_ref, v_ref, rq_ref, rk_ref, p_ref, mixed_ref, u1_ref, i1_ref, dg_ref, u2_ref, i2_ref,
):
    width = x_ref.shape[-1]
    head = width // (bias_ref.shape[1] // SPAN)
    per = LANES // head
    x = to_windows(x_ref[...].astype(F32))
    xb = x.astype(BF16)
    windows = x.shape[0] // SPAN
    sum_ones = block_ones(LANES, LANES, head, head)
    sum_ones = jnp.concatenate([sum_ones, sum_ones], 0)
    mask = block_ones(per * SPAN, LANES, SPAN, head)
    key_ones = block_ones(per * SPAN, per * SPAN, SPAN, SPAN)
    for g in range(width // LANES):
        at = slice(g * LANES, (g + 1) * LANES)
        q = dot(xb, w_qkv[:, at]).astype(BF16).astype(F32)
        k = dot(xb, w_qkv[:, width + g * LANES : width + (g + 1) * LANES]).astype(BF16).astype(F32)
        v = dot(xb, w_qkv[:, 2 * width + g * LANES : 2 * width + (g + 1) * LANES]).astype(BF16)
        q2 = split_dot(q * q, sum_ones)
        k2 = split_dot(k * k, sum_ones)
        rq = jnp.where(q2 > 1.0, lax.rsqrt(q2), 1.0)
        rk = jnp.where(k2 > 1.0, lax.rsqrt(k2), 1.0)
        rq_ref[:, at] = jnp.where(q2 == 1.0, -1.0, rq)
        rk_ref[:, at] = jnp.where(k2 == 1.0, -1.0, rk)
        qs = (q * rq * scale_ref[:, at]).astype(BF16)
        kn = (k * rk).astype(BF16)
        qs_ref[:, at] = qs
        kn_ref[:, at] = kn
        v_ref[:, at] = v
        bias = bias_ref[:, g * per * SPAN : (g + 1) * per * SPAN]
        for w in range(windows):
            rows = slice(w * SPAN, (w + 1) * SPAN)
            kb = jnp.concatenate([kn[rows]] * per, 0) * mask
            vb = jnp.concatenate([v[rows]] * per, 0) * mask
            expo = jnp.exp(dot(qs[rows], kb, NT) + bias)
            total = dot(expo.astype(BF16), key_ones)
            p = (expo / total).astype(BF16)
            p_ref[(g * windows + w) * SPAN : (g * windows + w + 1) * SPAN, :] = p
            mixed_ref[rows, at] = dot(p, vb).astype(BF16)
    u1, i1 = norm_parts(dot(mixed_ref[...], w_proj[...]))
    u1_ref[...] = u1
    i1_ref[...] = i1
    h1 = (x + u1 * gain_attn[...]).astype(BF16)
    mlp = jnp.zeros(x.shape, F32)
    step = width
    for c in range(w_fc1.shape[1] // step):
        cols = slice(c * step, (c + 1) * step)
        z = dot(h1, w_fc1[:, cols])
        zz = z * z
        t = jnp.tanh(GELU_A * z * (1.0 + GELU_B * zz))
        half = 0.5 * (1.0 + t)
        dg_ref[:, cols] = half + 0.5 * z * (1.0 - t * t) * (GELU_A + 3.0 * GELU_A * GELU_B * zz)
        mlp = mlp + dot((z * half).astype(BF16), w_fc2[cols, :])
    u2, i2 = norm_parts(mlp)
    u2_ref[...] = u2
    i2_ref[...] = i2
    out_ref[...] = from_windows(h1.astype(F32) + u2 * gain_mlp[...]).astype(BF16)


def unit_back(cot, unit, inv, sum_ones):
    along = split_dot(cot * unit, sum_ones)
    part = jnp.where(inv < 0.0, 0.5, jnp.where(inv < 1.0, 1.0, 0.0))
    return jnp.abs(inv) * (cot - part * unit * along)


def backward_kernel(
    cot_ref, w_qkv, w_proj, w_fc1, w_fc2, gain_attn, gain_mlp, scale_ref,
    qs_ref, kn_ref, v_ref, rq_ref, rk_ref, p_ref, mixed_ref, u1_ref, i1_ref, dg_ref, u2_ref, i2_ref,
    grad_ref, dm_ref,
):
    width = cot_ref.shape[-1]
    per = p_ref.shape[1] // SPAN
    head = LANES // per
    cot = to_windows(cot_ref[...].astype(F32))
    windows = cot.shape[0] // SPAN
    dmlp = norm_back(cot * gain_mlp[...], u2_ref[...], i2_ref[...]).astype(BF16)
    dh = jnp.zeros(cot.shape, F32)
    step = width
    for c in range(w_fc1.shape[1] // step):
        cols = slice(c * step, (c + 1) * step)
        dz = dot(dmlp, w_fc2[cols, :], NT) * dg_ref[:, cols]
        dh = dh + dot(dz.astype(BF16), w_fc1[:, cols], NT)
    dh = (cot + dh).astype(BF16).astype(F32)
    dproj = norm_back(dh * gain_attn[...], u1_ref[...], i1_ref[...]).astype(BF16)
    dm_ref[...] = dot(dproj, w_proj[...], NT).astype(BF16)
    sum_ones = block_ones(LANES, LANES, head, head)
    sum_ones = jnp.concatenate([sum_ones, sum_ones], 0)
    mask = block_ones(per * SPAN, LANES, SPAN, head)
    mask32 = mask.astype(F32)
    dx = dh
    for g in range(width // LANES):
        at = slice(g * LANES, (g + 1) * LANES)
        dm = dm_ref[:, at]
        own = (dm.astype(F32) * mixed_ref[:, at].astype(F32)).astype(BF16)
        both = jnp.concatenate([dm, own], 1)
        qs = qs_ref[:, at]
        kn = kn_ref[:, at]
        v = v_ref[:, at]
        dqs, dks, dvs = [], [], []
        for w in range(windows):
            rows = slice(w * SPAN, (w + 1) * SPAN)
            kb = jnp.concatenate([kn[rows]] * per, 0) * mask
            vb = jnp.concatenate([v[rows]] * per, 0) * mask
            p = p_ref[(g * windows + w) * SPAN : (g * windows + w + 1) * SPAN, :]
            spread = dot(both[rows], jnp.concatenate([vb, -mask], 1), NT)
            ds = (p.astype(F32) * spread).astype(BF16)
            dqs.append(dot(ds, kb))
            dkb = dot(ds, qs[rows], TN) * mask32
            dvb = dot(p, dm[rows], TN) * mask32
            dks.append(sum(dkb[i * SPAN : (i + 1) * SPAN] for i in range(per)))
            dvs.append(sum(dvb[i * SPAN : (i + 1) * SPAN] for i in range(per)))
        scale = scale_ref[:, at]
        dq = unit_back(
            jnp.concatenate(dqs, 0) * scale, qs.astype(F32) / scale, rq_ref[:, at], sum_ones
        )
        dk = unit_back(jnp.concatenate(dks, 0), kn.astype(F32), rk_ref[:, at], sum_ones)
        dv = jnp.concatenate(dvs, 0)
        dx = dx + dot(dq.astype(BF16), w_qkv[:, at], NT)
        dx = dx + dot(dk.astype(BF16), w_qkv[:, width + g * LANES : width + (g + 1) * LANES], NT)
        dx = dx + dot(dv.astype(BF16), w_qkv[:, 2 * width + g * LANES : 2 * width + (g + 1) * LANES], NT)
    grad_ref[...] = from_windows(dx).astype(BF16)


def order_kernel(tok_rows, tok_cols, row_devs, col_devs, feat_ref, patch_ref, cover_ref, w_ref, send_ref, pos_ref):
    slots, width = feat_ref.shape
    devs = row_devs * col_devs
    grid_cols = tok_cols * col_devs
    patch = patch_ref[...]
    row = patch // grid_cols
    col = patch % grid_cols
    target = row // tok_rows * col_devs + col // tok_cols
    hit = lax.broadcasted_iota(jnp.int32, (devs, slots), 0) == target
    i = lax.broadcasted_iota(jnp.int32, (slots, slots), 0)
    j = lax.broadcasted_iota(jnp.int32, (slots, slots), 1)
    earlier = jnp.where(i < j, 1.0, 0.0).astype(BF16)
    count = dot(jnp.where(hit, 1.0, 0.0).astype(BF16), earlier)
    rank = jnp.sum(jnp.where(hit, count, 0.0), 0, keepdims=True).astype(jnp.int32)
    pos = target * (slots // devs) + rank
    pos_ref[...] = pos
    place = jnp.where(i == pos, 1.0, 0.0).astype(BF16)
    query = dot(feat_ref[...], w_ref[...]).astype(BF16)
    send_ref[:, :width] = dot(place, query).astype(BF16)
    which = lax.broadcasted_iota(jnp.int32, (LANES, slots), 0)
    meta = jnp.where(which == 0, (row % tok_rows).astype(F32), 0.0)
    meta = jnp.where(which == 1, (col % tok_cols).astype(F32), meta)
    for c in range(3):
        meta = jnp.where(which == 2 + c, cover_ref[c : c + 1, :].astype(F32), meta)
    send_ref[:, width:] = dot(place, meta.astype(BF16), NT).astype(BF16)


def readout_kernel(cols, piece_ref, ext_ref, w_ref, scale_ref, head, out_ref, table_ref):
    width = out_ref.shape[1]
    rows = out_ref.shape[0]
    cells = ext_ref.shape[0]
    sum_ones = block_ones(LANES, LANES, head, head)
    sum_ones = jnp.concatenate([sum_ones, sum_ones], 0)

    @pl.when(pl.program_id(0) == 0)
    def _():
        for g in range(width // LANES):
            at = slice(g * LANES, (g + 1) * LANES)
            k = dot(ext_ref[...], w_ref[:, at]).astype(BF16).astype(F32)
            k2 = split_dot(k * k, sum_ones)
            table_ref[:, at] = (k * jnp.where(k2 > 1.0, lax.rsqrt(k2), 1.0)).astype(BF16)
        table_ref[:, width:] = dot(ext_ref[...], w_ref[:, width:]).astype(BF16)

    meta = piece_ref[:, width : width + LANES].astype(F32)
    base = (meta[:, 0:1] * cols + meta[:, 1:2]).astype(jnp.int32)
    lane = lax.broadcasted_iota(jnp.int32, (rows, cells), 1)
    picks = [
        jnp.where(lane == base + step, 1.0, 0.0).astype(BF16) for step in (0, 1, cols, cols + 1)
    ]
    flags = [None] + [meta[:, 2 + c : 3 + c] for c in range(3)]
    for g in range(width // LANES):
        at = slice(g * LANES, (g + 1) * LANES)
        q = piece_ref[:, at].astype(F32)
        q2 = split_dot(q * q, sum_ones)
        q = q * jnp.where(q2 > 1.0, lax.rsqrt(q2), 1.0) * scale_ref[:, at]
        both = jnp.concatenate([table_ref[:, at], table_ref[:, width + g * LANES : width + (g + 1) * LANES]], 1)
        total, mix = 0.0, 0.0
        for pick, flag in zip(picks, flags):
            got = dot(pick, both)
            expo = jnp.exp(split_dot(q * got[:, :LANES], sum_ones))
            if flag is not None:
                expo = expo * flag
            total = total + expo
            mix = mix + expo * got[:, LANES:]
        out_ref[:, at] = (mix / total).astype(BF16)


def finish_kernel(ret_ref, pos_ref, feat_ref, w_ref, live_ref, out_ref):
    slots = feat_ref.shape[0]
    i = lax.broadcasted_iota(jnp.int32, (slots, slots), 0)
    place = jnp.where(i == pos_ref[...], 1.0, 0.0).astype(BF16)
    mix = dot(place, ret_ref[...], TN).astype(BF16)
    updated = feat_ref[...].astype(F32) + dot(mix, w_ref[...])
    slot = lax.broadcasted_iota(jnp.int32, updated.shape, 0)
    out_ref[...] = jnp.where(slot < live_ref[0], updated, 0.0).astype(BF16)


def bias_index():
    grid_pos = np.stack(np.meshgrid(np.arange(WIN), np.arange(WIN), indexing="ij")).reshape(2, -1)
    offsets = grid_pos[:, :, None] - grid_pos[:, None, :] + WIN - 1
    return offsets[0] * (2 * WIN - 1) + offsets[1]


def moved(piece, rows, cols):
    n, m = lax.axis_size("gx"), lax.axis_size("gy")
    route = [
        (i * m + j, (i + rows) % n * m + (j + cols) % m) for i in range(n) for j in range(m)
    ]
    return lax.ppermute(piece, ("gx", "gy"), route)


def params(mib=48):
    return pltpu.CompilerParams(vmem_limit_bytes=mib * 1024 * 1024)


def local(
    wave_tokens, grad_out, w_qkv, w_proj, w_fc1, w_fc2, gain_attn, gain_mlp, attn_scale,
    bias_table, r_wq, r_wkv, r_wo, read_scale, floe_feat, floe_count, floe_patch, floe_cover,
):
    tok_rows, tok_cols, width = wave_tokens.shape
    heads = attn_scale.shape[0]
    head = width // heads
    tokens = tok_rows * tok_cols
    hidden = w_fc1.shape[1]
    row_devs, col_devs = lax.axis_size("gx"), lax.axis_size("gy")
    feat = floe_feat[0]
    slots = feat.shape[0]
    vmem = pl.BlockSpec(memory_space=pltpu.VMEM)
    s = SHIFT

    row_in = moved(jnp.concatenate([wave_tokens[:s, s:], grad_out[:s, s:]], 0), -1, 0)
    col_in = moved(jnp.concatenate([wave_tokens[s:, :s], grad_out[s:, :s]], 0), 0, -1)
    cor_in = moved(jnp.concatenate([wave_tokens[:s, :s], grad_out[:s, :s]], 0), -1, -1)

    def ahead(field, part):
        upper = jnp.concatenate([field[s:, s:], col_in[part * (tok_rows - s) : (part + 1) * (tok_rows - s)]], 1)
        lower = jnp.concatenate([row_in[part * s : (part + 1) * s], cor_in[part * s : (part + 1) * s]], 1)
        return jnp.concatenate([upper, lower], 0)

    send, pos = pl.pallas_call(
        lambda *refs: order_kernel(tok_rows, tok_cols, row_devs, col_devs, *refs),
        out_shape=(
            jax.ShapeDtypeStruct((slots, width + LANES), BF16),
            jax.ShapeDtypeStruct((1, slots), jnp.int32),
        ),
        in_specs=[vmem] * 4,
        out_specs=(vmem, vmem),
        compiler_params=params(),
        cost_estimate=pl.CostEstimate(flops=3000000000, bytes_accessed=3000000, transcendentals=0),
    )(feat, floe_patch, floe_cover[0], r_wq)
    piece = lax.all_to_all(send, ("gx", "gy"), split_axis=0, concat_axis=0, tiled=True)

    bias = bias_table[:, bias_index()].transpose(1, 0, 2).reshape(SPAN, heads * SPAN)
    scale = jnp.repeat(attn_scale, head)[None]
    gain_a, gain_m = gain_attn[None], gain_mlp[None]
    rolled = ahead(wave_tokens, 0)
    cot = ahead(grad_out, 1)
    wide = jax.ShapeDtypeStruct((tokens, width), BF16)
    wide32 = jax.ShapeDtypeStruct((tokens, width), F32)
    one = jax.ShapeDtypeStruct((tokens, 1), F32)
    res = pl.pallas_call(
        forward_kernel,
        out_shape=(
            jax.ShapeDtypeStruct(wave_tokens.shape, BF16),
            wide, wide, wide, wide32, wide32,
            jax.ShapeDtypeStruct((tokens * width // LANES, LANES // head * SPAN), BF16),
            wide, wide32, one, jax.ShapeDtypeStruct((tokens, hidden), F32), wide32, one,
        ),
        in_specs=[vmem] * 9,
        out_specs=(vmem,) * 13,
        compiler_params=params(),
        cost_estimate=pl.CostEstimate(flops=8000000000, bytes_accessed=8000000, transcendentals=1000000),
    )(rolled, w_qkv, w_proj, w_fc1, w_fc2, gain_a, gain_m, scale, bias)
    out = res[0]
    near, far = tok_rows - s + 1, tok_cols - s
    row_out = moved(out[s:, : far + 1], 1, 0)
    col_out = moved(out[:near, far:], 0, 1)
    cor_out = moved(out[s:, far:], 1, 1)
    grad = pl.pallas_call(
        backward_kernel,
        out_shape=jax.ShapeDtypeStruct(wave_tokens.shape, BF16),
        in_specs=[vmem] * 20,
        out_specs=vmem,
        scratch_shapes=[pltpu.VMEM((tokens, width), BF16)],
        compiler_params=params(),
        cost_estimate=pl.CostEstimate(flops=10000000000, bytes_accessed=8000000, transcendentals=0),
    )(cot, w_qkv, w_proj, w_fc1, w_fc2, gain_a, gain_m, scale, *res[1:])
    row_grad = moved(grad[s:, :far], 1, 0)
    col_grad = moved(grad[: tok_rows - s, far:], 0, 1)
    cor_grad = moved(grad[s:, far:], 1, 1)

    ext = jnp.concatenate(
        [
            jnp.concatenate([cor_out, row_out], 1),
            jnp.concatenate([col_out, out[:near, : far + 1]], 1),
        ],
        0,
    )
    patch_out = ext[:tok_rows, :tok_cols]
    ext_cols = tok_cols + 1
    cells = (tok_rows + 1) * ext_cols
    padded = -(-cells // LANES) * LANES
    table = jnp.pad(ext.reshape(cells, width), ((0, padded - cells), (0, 0)))
    parts = 3
    chunk = slots // parts
    mix = pl.pallas_call(
        lambda a, b, c, d, e, f: readout_kernel(ext_cols, a, b, c, d, head, e, f),
        out_shape=jax.ShapeDtypeStruct((slots, width), BF16),
        grid=(parts,),
        in_specs=[
            pl.BlockSpec((chunk, width + LANES), lambda i: (i, 0)),
            vmem, vmem, vmem,
        ],
        out_specs=pl.BlockSpec((chunk, width), lambda i: (i, 0)),
        scratch_shapes=[pltpu.VMEM((padded, 2 * width), BF16)],
        compiler_params=params(),
        cost_estimate=pl.CostEstimate(flops=8000000000, bytes_accessed=3000000, transcendentals=1000000),
    )(piece, table, r_wkv, jnp.repeat(read_scale, head)[None])
    back = lax.all_to_all(mix, ("gx", "gy"), split_axis=0, concat_axis=0, tiled=True)
    floe_out = pl.pallas_call(
        finish_kernel,
        out_shape=jax.ShapeDtypeStruct((slots, width), BF16),
        in_specs=[vmem] * 4 + [pl.BlockSpec(memory_space=pltpu.SMEM)],
        out_specs=vmem,
        compiler_params=params(),
        cost_estimate=pl.CostEstimate(flops=1500000000, bytes_accessed=3000000, transcendentals=0),
    )(back, pos, feat, r_wo, floe_count)
    grad_in = jnp.concatenate(
        [
            jnp.concatenate([cor_grad, row_grad], 1),
            jnp.concatenate([col_grad, grad[: tok_rows - s, :far]], 1),
        ],
        0,
    )
    return (patch_out, grad_in, floe_out[None])


def solution(mesh):
    grid = P("gx", "gy", None)
    owner = ("gx", "gy")
    in_specs = (grid, grid) + (P(),) * 12 + (P(owner, None, None), P(owner), P(owner, None), P(owner, None, None))
    out_specs = (grid, grid, P(owner, None, None))
    return jax.shard_map(local, mesh=mesh, in_specs=in_specs, out_specs=out_specs, check_vma=False)
```

profile of v0, /device:TPU:0, one launch (start us, length us, event | category | flops | bytes accessed | tf_op | source)
XLA Modules:
  0.0 116.8 jit_solution(12687625486850138824)
XLA Ops:
  1.5 6.4 %collective-permute-start.2 = (bf16[8,4,512]{2,1,0:T(4,128)(2,1)S(1)}, bf16[8,4,512]{2,1,0:T(4,128)(2,1)S(1)}, u32[]{:S(2)}, u32[]{:S(2)}) collective-permute-start(bf16[8,4,512]{2,1,0:T(4,128)(2,1)S(1)} %pad_maximum_fusion.2), channel_id=1, source_target_pairs={{0,31},{1,28},{2,29},{3,30},{4,3},{5,0},{6,1},{7,2},{8,7},{9,4},{1... | collective-permute-start | bytes 98312 | tf_op jit(solution)/shard_map/ppermute | solution.py:275
  7.9 1.2 %fusion.2 = (bf16[4,28,512]{2,1,0:T(8,128)(2,1)S(1)}, bf16[4,28,512]{2,1,0:T(8,128)(2,1)S(1)}, bf16[4,28,512]{2,1,0:T(8,128)(2,1)S(1)}, bf16[4,28,512]{2,1,0:T(8,128)(2,1)S(1)}) fusion(bf16[8,32,512]{2,1,0:T(8,128)(2,1)} %param.21, bf16[8,32,512]{2,1,0:T(8,128)(2,1)} %param.20), kind=kLoop, calls=%fused_computation.12 | loop fusion | bytes 917504 | tf_op jit(solution)/shard_map/slice | solution.py:302
  11.4 1.1 copy-done.1
  12.5 1.0 copy-done.3
  14.3 2.9 %shard_map.213 = (bf16[768,640]{1,0:T(8,128)(2,1)}, s32[1,768]{1,0:T(1,128)S(1)}) custom-call(bf16[768,512]{1,0:T(8,128)(2,1)S(1)} %bitcast.16, s32[1,768]{1,0:T(1,128)S(1)} %copy-done.6, s32[3,768]{1,0:T(4,128)S(1)} %bitcast.15, bf16[512,512]{1,0:T(8,128)(2,1)S(1)} %copy-done.3), custom_call_target="tpu_custom_call" | custom-call | flops 3000000000 | bytes 3000000 | tf_op jit(solution)/shard_map/pallas_call | solution.py:306
  17.2 2.6 %all-to-all-start = ((bf16[32,24,640]{2,1,0:T(8,128)(2,1)}), bf16[32,24,640]{2,1,0:T(8,128)(2,1)S(1)}, u32[]{:S(2)}, u32[]{:S(2)}) async-start(bf16[32,24,640]{2,1,0:T(8,128)(2,1)} %bitcast.5), calls=%async_computation | async-start | bytes 1966080 | tf_op jit(solution)/shard_map/all_to_all | solution.py:317
  20.1 14.2 %gather_fusion = f32[4096,16]{1,0:T(8,128)} fusion(f32[16,225]{0,1:T(8,128)S(1)} %copy.23, s32[4096]{0:T(1024)S(1)} %broadcast_clamp_fusion), kind=kCustom, calls=%fused_computation | custom fusion | bytes 540672 | tf_op jit(solution)/shard_map/gather | solution.py:319
  34.3 2.2 %copy.24 = f32[64,64,16]{1,2,0:T(8,128)S(1)} copy(f32[64,64,16]{2,1,0:T(8,128)} %bitcast.22) | data formatting | bytes 524288 | tf_op jit(solution)/shard_map/gather | solution.py:319
  37.0 11.1 %shard_map.211 = (bf16[8,32,512]{2,1,0:T(8,128)(2,1)S(1)}, bf16[256,512]{1,0:T(8,128)(2,1)S(1)}, bf16[256,512]{1,0:T(8,128)(2,1)S(1)}, bf16[256,512]{1,0:T(8,128...) custom-call(bf16[8,32,512]{2,1,0:T(8,128)(2,1)S(1)} %maximum_maximum, ...), custom_call_target="tpu_custom_call" | custom-call | flops 8000000000 | bytes 8000000 | tf_op jit(solution)/shard_map/pallas_call | solution.py:327
  53.4 1.7 %collective-permute-start.5 = (bf16[5,4,512]{2,1,0:T(4,128)(2,1)S(1)}, bf16[5,4,512]{2,1,0:T(4,128)(2,1)S(1)}, u32[]{:S(2)}, u32[]{:S(2)}) collective-permute-start(bf16[5,4,512]{2,1,0:T(4,128)(2,1)S(1)} %slice.81), channel_id=1, source_target_pairs={{0,1},{1,2},{2,3},{3,0},{4,5},{5,6},{6,7},{7,4},{8,9},{9,10},{10,1... | collective-permute-start | bytes 61448 | tf_op jit(solution)/shard_map/ppermute | solution.py:275
  55.0 2.7 %collective-permute-start.3 = (bf16[4,4,512]{2,1,0:T(4,128)(2,1)S(1)}, bf16[4,4,512]{2,1,0:T(4,128)(2,1)S(1)}, u32[]{:S(2)}, u32[]{:S(2)}) collective-permute-start(bf16[4,4,512]{2,1,0:T(4,128)(2,1)S(1)} %slice.79), channel_id=1, source_target_pairs={{0,5},{1,6},{2,7},{3,4},{4,9},{5,10},{6,11},{7,8},{8,13},{9,14},{1... | collective-permute-start | bytes 49160 | tf_op jit(solution)/shard_map/ppermute | solution.py:275
  57.8 4.3 %collective-permute-done.3 = bf16[4,4,512]{2,1,0:T(4,128)(2,1)S(1)} collective-permute-done((bf16[4,4,512]{2,1,0:T(4,128)(2,1)S(1)}, bf16[4,4,512]{2,1,0:T(4,128)(2,1)S(1)}, u32[]{:S(2)}, u32[]{:S(2)}) %collective-permute-start.3) | collective-permute-done | bytes 16416 | tf_op jit(solution)/shard_map/ppermute | solution.py:275
  64.9 15.5 %shard_map.214 = bf16[768,512]{1,0:T(8,128)(2,1)} custom-call(bf16[768,640]{1,0:T(8,128)(2,1)S(1)} %bitcast.13, bf16[384,512]{1,0:T(8,128)(2,1)S(1)} %pad.4.b, bf16[512,1024]{1,0:T(8,128)(2,1)S(1)} %copy-done, f32[1,512]{1,0:T(1,128)S(1)} %broadcast_in_dim_reshape.7.d), custom_call_target="tpu_custom_call" | custom-call | flops 8000000000 | bytes 3000000 | tf_op jit(solution)/shard_map/pallas_call | solution.py:372
  80.3 3.1 %all-to-all-start.1 = ((bf16[32,24,512]{2,1,0:T(8,128)(2,1)}), bf16[32,24,512]{2,1,0:T(8,128)(2,1)S(1)}, u32[]{:S(2)}, u32[]{:S(2)}) async-start(bf16[32,24,512]{2,1,0:T(8,128)(2,1)} %bitcast.7), calls=%async_computation.1 | async-start | bytes 1572864 | tf_op jit(solution)/shard_map/all_to_all | solution.py:385
  83.5 1.0 copy-done.10
  84.5 1.0 copy-done.12
  85.6 1.0 copy-done.14
  86.6 1.0 copy-done.16
  87.6 1.0 copy-done.18
  93.4 11.0 %shard_map.212 = bf16[8,32,512]{2,1,0:T(8,128)(2,1)S(1)} custom-call(bf16[8,32,512]{2,1,0:T(8,128)(2,1)S(1)} %maximum_maximum_fusion.2.cot_ref, bf16[512,1536]{1,0:T(8,128)(2,1)} %w_qkv.3, bf16[512,512]{1,0:T(8,128)(2,1)S(1)} %copy-done.4, bf16[512,2048]{1,0:T(8,128)(2,1)} %w_fc1.3, bf16[2048,512]{1,0:T(8,128)(2,1)} %w_fc2.3, f32[1,512]{1,0:T(1,128)S(1)} %bitcast.19, ...), custom_call_target="tpu_custom_call" | custom-call | flops 10000000000 | bytes 8000000 | tf_op jit(solution)/shard_map/pallas_call | solution.py:345
  104.7 1.7 %collective-permute-start.8 = (bf16[4,4,512]{2,1,0:T(4,128)(2,1)S(1)}, bf16[4,4,512]{2,1,0:T(4,128)(2,1)S(1)}, u32[]{:S(2)}, u32[]{:S(2)}) collective-permute-start(bf16[4,4,512]{2,1,0:T(4,128)(2,1)S(1)} %get-tuple-element.34), channel_id=1, source_target_pairs={{0,1},{1,2},{2,3},{3,0},{4,5},{5,6},{6,7},{7,4},{8,9},{9,10},{10,1... | collective-permute-start | bytes 49160 | tf_op jit(solution)/shard_map/ppermute | solution.py:275
  106.4 2.2 %collective-permute-start.6 = (bf16[4,4,512]{2,1,0:T(4,128)(2,1)S(1)}, bf16[4,4,512]{2,1,0:T(4,128)(2,1)S(1)}, u32[]{:S(2)}, u32[]{:S(2)}) collective-permute-start(bf16[4,4,512]{2,1,0:T(4,128)(2,1)S(1)} %get-tuple-element.33), channel_id=1, source_target_pairs={{0,5},{1,6},{2,7},{3,4},{4,9},{5,10},{6,11},{7,8},{8,13},{9,14},{1... | collective-permute-start | bytes 49160 | tf_op jit(solution)/shard_map/ppermute | solution.py:275
  109.4 3.8 %collective-permute-done.6 = bf16[4,4,512]{2,1,0:T(4,128)(2,1)S(1)} collective-permute-done((bf16[4,4,512]{2,1,0:T(4,128)(2,1)S(1)}, bf16[4,4,512]{2,1,0:T(4,128)(2,1)S(1)}, u32[]{:S(2)}, u32[]{:S(2)}) %collective-permute-start.6) | collective-permute-done | bytes 16416 | tf_op jit(solution)/shard_map/ppermute | solution.py:275
  114.7 2.1 %shard_map.215 = bf16[768,512]{1,0:T(8,128)(2,1)} custom-call(bf16[768,512]{1,0:T(8,128)(2,1)S(1)} %bitcast.14, s32[1,768]{1,0:T(1,128)S(1)} %get-tuple-element.32.pos_ref, bf16[768,512]{1,0:T(8,128)(2,1)S(1)} %bitcast.17, bf16[512,512]{1,0:T(8,128)(2,1)S(1)} %copy-done.5, s32[1]{0:T(128)S(6)} %copy.28.live_ref), custom_call_target="tpu_custom_call" | custom-call | flops 1500000000 | bytes 3000000 | tf_op jit(solution)/shard_map/pallas_call | solution.py:386
  (104 shorter events, 19.1 us)
Async XLA Ops:
  1.5 35.3 %collective-permute-start.2 = (bf16[8,4,512]{2,1,0:T(4,128)(2,1)S(1)}, bf16[8,4,512]{2,1,0:T(4,128)(2,1)S(1)}, u32[]{:S(2)}, u32[]{:S(2)}) collective-permute-start(bf16[8,4,512]{2,1,0:T(4,128)(2,1)S(1)} %pad_maximum_fusion.2), channel_id=1, source_target_pairs={{0,31},{1,28},{2,29},{3,30},{4,3},{5,0},{6,1},{7,2},{8,7},{9,4},{1... | collective-permute-start | bytes 98312 | tf_op jit(solution)/shard_map/ppermute | solution.py:275
  9.2 27.7 %collective-permute-start.1 = (bf16[8,28,512]{2,1,0:T(8,128)(2,1)S(1)}, bf16[8,28,512]{2,1,0:T(8,128)(2,1)S(1)}, u32[]{:S(2)}, u32[]{:S(2)}) collective-permute-start(bf16[8,28,512]{2,1,0:T(8,128)(2,1)S(1)} %pad_maximum_fusion), channel_id=1, source_target_pairs={{0,28},{1,29},{2,30},{3,31},{4,0},{5,1},{6,2},{7,3},{8,4},{9,5},{1... | collective-permute-start | bytes 688136 | tf_op jit(solution)/shard_map/ppermute | solution.py:275
  10.1 26.8 %collective-permute-start = (bf16[8,4,512]{2,1,0:T(4,128)(2,1)S(1)}, bf16[8,4,512]{2,1,0:T(4,128)(2,1)S(1)}, u32[]{:S(2)}, u32[]{:S(2)}) collective-permute-start(bf16[8,4,512]{2,1,0:T(4,128)(2,1)S(1)} %pad_maximum_fusion.1), channel_id=1, source_target_pairs={{0,3},{1,0},{2,1},{3,2},{4,7},{5,4},{6,5},{7,6},{8,11},{9,8},{10,9... | collective-permute-start | bytes 98312 | tf_op jit(solution)/shard_map/ppermute | solution.py:275
  14.3 5.5 %copy-start.32 = (s32[4096]{0:T(1024)S(1)}, s32[4096]{0:T(1024)}, u32[]{:S(2)}) copy-start(s32[4096]{0:T(1024)} %constant.18) | copy-start | bytes 49156
  14.3 5.6 %copy-start.33 = (f32[16]{0:T(128)S(1)}, f32[16]{0:T(128)}, u32[]{:S(2)}) copy-start(f32[16]{0:T(128)} %param.28) | copy-start | bytes 196
  14.3 5.7 %copy-start.31 = (f32[16,225]{1,0:T(8,128)S(1)}, f32[16,225]{1,0:T(8,128)}, u32[]{:S(2)}) copy-start(f32[16,225]{1,0:T(8,128)} %param.29) | copy-start | bytes 43204
  17.2 47.7 %all-to-all-start = ((bf16[32,24,640]{2,1,0:T(8,128)(2,1)}), bf16[32,24,640]{2,1,0:T(8,128)(2,1)S(1)}, u32[]{:S(2)}, u32[]{:S(2)}) async-start(bf16[32,24,640]{2,1,0:T(8,128)(2,1)} %bitcast.5), calls=%async_computation | async-start | bytes 1966080 | tf_op jit(solution)/shard_map/all_to_all | solution.py:317
  34.3 2.7 %copy-start.4 = (bf16[512,512]{1,0:T(8,128)(2,1)S(1)}, bf16[512,512]{1,0:T(8,128)(2,1)}, u32[]{:S(2)}) copy-start(bf16[512,512]{1,0:T(8,128)(2,1)} %w_proj.3) | copy-start | bytes 1572868
  34.3 2.7 %copy-start.7 = (f32[512]{0:T(512)S(1)}, f32[512]{0:T(512)}, u32[]{:S(2)}) copy-start(f32[512]{0:T(512)} %param.26) | copy-start | bytes 6148
  34.3 2.7 %copy-start.8 = (f32[512]{0:T(512)S(1)}, f32[512]{0:T(512)}, u32[]{:S(2)}) copy-start(f32[512]{0:T(512)} %param.27) | copy-start | bytes 6148
  53.3 4.6 %copy-start.9 = (f32[256,512]{1,0:T(8,128)}, f32[256,512]{1,0:T(8,128)S(1)}, u32[]{:S(2)}) copy-start(f32[256,512]{1,0:T(8,128)S(1)} %get-tuple-element.22.rq_ref) | copy-start | bytes 1572868
  53.3 8.9 %copy-start.11 = (f32[256,512]{1,0:T(8,128)}, f32[256,512]{1,0:T(8,128)S(1)}, u32[]{:S(2)}) copy-start(f32[256,512]{1,0:T(8,128)S(1)} %get-tuple-element.23.rk_ref) | copy-start | bytes 1572868
  53.3 8.9 %copy-start.25 = (f32[256,1]{1,0:T(8,128)}, f32[256,1]{1,0:T(8,128)S(1)}, u32[]{:S(2)}) copy-start(f32[256,1]{1,0:T(8,128)S(1)} %get-tuple-element.27.i1_ref) | copy-start | bytes 3076
  53.3 11.6 %copy-start = (bf16[512,1024]{1,0:T(8,128)(2,1)S(1)}, bf16[512,1024]{1,0:T(8,128)(2,1)}, u32[]{:S(2)}) copy-start(bf16[512,1024]{1,0:T(8,128)(2,1)} %c.1) | copy-start | bytes 3145732
  53.4 8.8 %collective-permute-start.5 = (bf16[5,4,512]{2,1,0:T(4,128)(2,1)S(1)}, bf16[5,4,512]{2,1,0:T(4,128)(2,1)S(1)}, u32[]{:S(2)}, u32[]{:S(2)}) collective-permute-start(bf16[5,4,512]{2,1,0:T(4,128)(2,1)S(1)} %slice.81), channel_id=1, source_target_pairs={{0,1},{1,2},{2,3},{3,0},{4,5},{5,6},{6,7},{7,4},{8,9},{9,10},{10,1... | collective-permute-start | bytes 61448 | tf_op jit(solution)/shard_map/ppermute | solution.py:275
  55.0 7.1 %collective-permute-start.4 = (bf16[4,29,512]{2,1,0:T(8,128)(2,1)S(1)}, bf16[4,29,512]{2,1,0:T(8,128)(2,1)S(1)}, u32[]{:S(2)}, u32[]{:S(2)}) collective-permute-start(bf16[4,29,512]{2,1,0:T(8,128)(2,1)S(1)} %slice.80), channel_id=1, source_target_pairs={{0,4},{1,5},{2,6},{3,7},{4,8},{5,9},{6,10},{7,11},{8,12},{9,13},{1... | collective-permute-start | bytes 356360 | tf_op jit(solution)/shard_map/ppermute | solution.py:275
  55.0 7.1 %collective-permute-start.3 = (bf16[4,4,512]{2,1,0:T(4,128)(2,1)S(1)}, bf16[4,4,512]{2,1,0:T(4,128)(2,1)S(1)}, u32[]{:S(2)}, u32[]{:S(2)}) collective-permute-start(bf16[4,4,512]{2,1,0:T(4,128)(2,1)S(1)} %slice.79), channel_id=1, source_target_pairs={{0,5},{1,6},{2,7},{3,4},{4,9},{5,10},{6,11},{7,8},{8,13},{9,14},{1... | collective-permute-start | bytes 49160 | tf_op jit(solution)/shard_map/ppermute | solution.py:275
  80.3 34.4 %all-to-all-start.1 = ((bf16[32,24,512]{2,1,0:T(8,128)(2,1)}), bf16[32,24,512]{2,1,0:T(8,128)(2,1)S(1)}, u32[]{:S(2)}, u32[]{:S(2)}) async-start(bf16[32,24,512]{2,1,0:T(8,128)(2,1)} %bitcast.7), calls=%async_computation.1 | async-start | bytes 1572864 | tf_op jit(solution)/shard_map/all_to_all | solution.py:385
  93.3 20.6 %copy-start.30 = (bf16[9,33,512]{2,1,0:T(8,128)(2,1)S(1)}, bf16[9,33,512]{2,1,0:T(8,128)(2,1)}, u32[]{:S(2)}) copy-start(bf16[9,33,512]{2,1,0:T(8,128)(2,1)} %copy-done.29) | copy-start | bytes 912388
  93.4 21.4 %copy-start.2 = (bf16[1,768,512]{2,1,0:T(8,128)(2,1)S(1)}, bf16[1,768,512]{2,1,0:T(8,128)(2,1)}, u32[]{:S(2)}) copy-start(bf16[1,768,512]{2,1,0:T(8,128)(2,1)} %param.34) | copy-start | bytes 2359300
  93.4 21.4 %copy-start.5 = (bf16[512,512]{1,0:T(8,128)(2,1)S(1)}, bf16[512,512]{1,0:T(8,128)(2,1)}, u32[]{:S(2)}) copy-start(bf16[512,512]{1,0:T(8,128)(2,1)} %w_ref.1) | copy-start | bytes 1572868
  104.4 8.8 %collective-permute-start.7 = (bf16[4,28,512]{2,1,0:T(8,128)(2,1)S(1)}, bf16[4,28,512]{2,1,0:T(8,128)(2,1)S(1)}, u32[]{:S(2)}, u32[]{:S(2)}) collective-permute-start(bf16[4,28,512]{2,1,0:T(8,128)(2,1)S(1)} %get-tuple-element.35), channel_id=1, source_target_pairs={{0,4},{1,5},{2,6},{3,7},{4,8},{5,9},{6,10},{7,11},{8,12},{9,13},{1... | collective-permute-start | bytes 344072 | tf_op jit(solution)/shard_map/ppermute | solution.py:275
  104.7 4.7 %collective-permute-start.8 = (bf16[4,4,512]{2,1,0:T(4,128)(2,1)S(1)}, bf16[4,4,512]{2,1,0:T(4,128)(2,1)S(1)}, u32[]{:S(2)}, u32[]{:S(2)}) collective-permute-start(bf16[4,4,512]{2,1,0:T(4,128)(2,1)S(1)} %get-tuple-element.34), channel_id=1, source_target_pairs={{0,1},{1,2},{2,3},{3,0},{4,5},{5,6},{6,7},{7,4},{8,9},{9,10},{10,1... | collective-permute-start | bytes 49160 | tf_op jit(solution)/shard_map/ppermute | solution.py:275
  106.4 6.8 %collective-permute-start.6 = (bf16[4,4,512]{2,1,0:T(4,128)(2,1)S(1)}, bf16[4,4,512]{2,1,0:T(4,128)(2,1)S(1)}, u32[]{:S(2)}, u32[]{:S(2)}) collective-permute-start(bf16[4,4,512]{2,1,0:T(4,128)(2,1)S(1)} %get-tuple-element.33), channel_id=1, source_target_pairs={{0,5},{1,6},{2,7},{3,4},{4,9},{5,10},{6,11},{7,8},{8,13},{9,14},{1... | collective-permute-start | bytes 49160 | tf_op jit(solution)/shard_map/ppermute | solution.py:275
  (22 other events, 21.1 us)
where the time goes:
time: 118 us; the launch traced here: 117 us
  Pallas kernels  42.6 us (36%)
  local copies, waits for them, and re-layouts  41.1 us (35%)
  starting transfers between devices  22.3 us (19%)
  waiting for transfers between devices  8.2 us (7%)
  between operations  1.59 us (1%)
    unnamed x72, local copies, waits for them, and re-layouts  19.5 us
    ppermute x9, starting transfers between devices, moved(): return lax.ppermute(piece, ('gx', 'gy'), route)  16.6 us
    gather x2, local copies, waits for them, and re-layouts, local(): bias_table[:, bias_index()].transpose(1, 0, 2).reshape(SPAN, heads * SPAN)  16.4 us
    pallas_call x1, Pallas kernels, local(): pl.pallas_call(lambda a, b, c, d, e, f: readout_kernel(ext_cols, a, b, c,...  15.5 us
    pallas_call x1, Pallas kernels, local(): pl.pallas_call(forward_kernel, out_shape=(jax.ShapeDtypeStruct(wave_token...  11.1 us
    pallas_call x1, Pallas kernels, local(): pl.pallas_call(backward_kernel, out_shape=jax.ShapeDtypeStruct(wave_token...  11 us
    ppermute x9, waiting for transfers between devices, moved(): return lax.ppermute(piece, ('gx', 'gy'), route)  8.2 us
    all_to_all x1, starting transfers between devices, local(): lax.all_to_all(mix, ('gx', 'gy'), split_axis=0, concat_axis=0, tiled=True)  3.14 us
  transfers between devices with their start and end apart: 11, of which 3 were waited for; matrix products, arithmetic and copies ran while one was open for 19% of the time, Pallas kernels for 21%

commit v1 on v0

--- a/solution.py
+++ b/solution.py
@@ -1,6 +1,5 @@
 import jax
 import jax.numpy as jnp
-import numpy as np
 from jax import lax
 from jax.experimental import pallas as pl
 from jax.experimental.pallas import tpu as pltpu
@@ -91,15 +90,18 @@
         kn_ref[:, at] = kn
         v_ref[:, at] = v
         bias = bias_ref[:, g * per * SPAN : (g + 1) * per * SPAN]
+        expo = []
         for w in range(windows):
             rows = slice(w * SPAN, (w + 1) * SPAN)
             kb = jnp.concatenate([kn[rows]] * per, 0) * mask
+            expo.append(jnp.exp(dot(qs[rows], kb, NT) + bias))
+        expo = jnp.concatenate(expo, 0)
+        p = (expo / dot(expo.astype(BF16), key_ones)).astype(BF16)
+        p_ref[g * windows * SPAN : (g + 1) * windows * SPAN, :] = p
+        for w in range(windows):
+            rows = slice(w * SPAN, (w + 1) * SPAN)
             vb = jnp.concatenate([v[rows]] * per, 0) * mask
-            expo = jnp.exp(dot(qs[rows], kb, NT) + bias)
-            total = dot(expo.astype(BF16), key_ones)
-            p = (expo / total).astype(BF16)
-            p_ref[(g * windows + w) * SPAN : (g * windows + w + 1) * SPAN, :] = p
-            mixed_ref[rows, at] = dot(p, vb).astype(BF16)
+            mixed_ref[rows, at] = dot(p[rows], vb).astype(BF16)
     u1, i1 = norm_parts(dot(mixed_ref[...], w_proj[...]))
     u1_ref[...] = u1
     i1_ref[...] = i1
@@ -112,7 +114,8 @@
         zz = z * z
         t = jnp.tanh(GELU_A * z * (1.0 + GELU_B * zz))
         half = 0.5 * (1.0 + t)
-        dg_ref[:, cols] = half + 0.5 * z * (1.0 - t * t) * (GELU_A + 3.0 * GELU_A * GELU_B * zz)
+        slope = GELU_A + 3.0 * GELU_A * GELU_B * zz
+        dg_ref[:, cols] = (half + 0.5 * z * (1.0 - t * t) * slope).astype(BF16)
         mlp = mlp + dot((z * half).astype(BF16), w_fc2[cols, :])
     u2, i2 = norm_parts(mlp)
     u2_ref[...] = u2
@@ -141,7 +144,7 @@
     step = width
     for c in range(w_fc1.shape[1] // step):
         cols = slice(c * step, (c + 1) * step)
-        dz = dot(dmlp, w_fc2[cols, :], NT) * dg_ref[:, cols]
+        dz = dot(dmlp, w_fc2[cols, :], NT) * dg_ref[:, cols].astype(F32)
         dh = dh + dot(dz.astype(BF16), w_fc1[:, cols], NT)
     dh = (cot + dh).astype(BF16).astype(F32)
     dproj = norm_back(dh * gain_attn[...], u1_ref[...], i1_ref[...]).astype(BF16)
@@ -230,24 +233,26 @@
     meta = piece_ref[:, width : width + LANES].astype(F32)
     base = (meta[:, 0:1] * cols + meta[:, 1:2]).astype(jnp.int32)
     lane = lax.broadcasted_iota(jnp.int32, (rows, cells), 1)
-    picks = [
-        jnp.where(lane == base + step, 1.0, 0.0).astype(BF16) for step in (0, 1, cols, cols + 1)
-    ]
-    flags = [None] + [meta[:, 2 + c : 3 + c] for c in range(3)]
+    picks = jnp.concatenate(
+        [jnp.where(lane == base + step, 1.0, 0.0).astype(BF16) for step in (0, 1, cols, cols + 1)], 0
+    )
+    flags = [jnp.broadcast_to(meta[:, 2 + c : 3 + c], (rows, LANES)) for c in range(3)]
     for g in range(width // LANES):
         at = slice(g * LANES, (g + 1) * LANES)
         q = piece_ref[:, at].astype(F32)
         q2 = split_dot(q * q, sum_ones)
         q = q * jnp.where(q2 > 1.0, lax.rsqrt(q2), 1.0) * scale_ref[:, at]
         both = jnp.concatenate([table_ref[:, at], table_ref[:, width + g * LANES : width + (g + 1) * LANES]], 1)
+        got = dot(picks, both)
+        scores = split_dot(jnp.concatenate([q] * 4, 0) * got[:, :LANES], sum_ones)
         total, mix = 0.0, 0.0
-        for pick, flag in zip(picks, flags):
-            got = dot(pick, both)
-            expo = jnp.exp(split_dot(q * got[:, :LANES], sum_ones))
-            if flag is not None:
-                expo = expo * flag
+        for c in range(4):
+            at_c = slice(c * rows, (c + 1) * rows)
+            expo = jnp.exp(scores[at_c])
+            if c > 0:
+                expo = expo * flags[c - 1]
             total = total + expo
-            mix = mix + expo * got[:, LANES:]
+            mix = mix + expo * got[at_c, LANES:]
         out_ref[:, at] = (mix / total).astype(BF16)
 
 
@@ -261,10 +266,36 @@
     out_ref[...] = jnp.where(slot < live_ref[0], updated, 0.0).astype(BF16)
 
 
-def bias_index():
-    grid_pos = np.stack(np.meshgrid(np.arange(WIN), np.arange(WIN), indexing="ij")).reshape(2, -1)
-    offsets = grid_pos[:, :, None] - grid_pos[:, None, :] + WIN - 1
-    return offsets[0] * (2 * WIN - 1) + offsets[1]
+def bias_kernel(table_ref, out_ref):
+    size, lanes = table_ref.shape
+    heads = lanes // WIN
+    table = table_ref[...]
+    high = table.astype(BF16)
+    low = (table - high.astype(F32)).astype(BF16)
+    m_b = lax.broadcasted_iota(jnp.int32, (2 * SPAN, size), 0)
+    entry = lax.broadcasted_iota(jnp.int32, (2 * SPAN, size), 1)
+    start = m_b // WIN * (2 * WIN - 1) + m_b % WIN + WIN - 1
+    lane_d = lax.broadcasted_iota(jnp.int32, (size, lanes), 1) // heads
+    edge = jnp.zeros((2 * SPAN, 2 * lanes), F32)
+    for d in range(WIN):
+        pick = jnp.where(entry == start - d, 1.0, 0.0).astype(BF16)
+        here = jnp.where(lane_d == d, 1.0, 0.0).astype(BF16)
+        edge = edge + dot(pick, jnp.concatenate([high * here, low * here], 1))
+    rows = [edge[(WIN - 1 - c) * WIN : (WIN - 1 - c) * WIN + SPAN, :] for c in range(WIN)]
+    both = jnp.concatenate(
+        [
+            jnp.concatenate([row[:, :lanes] for row in rows], 1),
+            jnp.concatenate([row[:, lanes:] for row in rows], 1),
+        ],
+        0,
+    ).astype(BF16)
+    step = 2 * LANES
+    source = lax.broadcasted_iota(jnp.int32, (WIN * lanes, step), 0)
+    for part in range(heads * SPAN // step):
+        col = lax.broadcasted_iota(jnp.int32, (1, step), 1) + part * step
+        want = col // WIN % WIN * lanes + col % WIN * heads + col // SPAN
+        got = dot(both, jnp.where(source == want, 1.0, 0.0).astype(BF16))
+        out_ref[:, part * step : (part + 1) * step] = got[:SPAN] + got[SPAN:]
 
 
 def moved(piece, rows, cols):
@@ -275,7 +306,7 @@
     return lax.ppermute(piece, ("gx", "gy"), route)
 
 
-def params(mib=48):
+def params(mib=24):
     return pltpu.CompilerParams(vmem_limit_bytes=mib * 1024 * 1024)
 
 
@@ -316,7 +347,14 @@
     )(feat, floe_patch, floe_cover[0], r_wq)
     piece = lax.all_to_all(send, ("gx", "gy"), split_axis=0, concat_axis=0, tiled=True)
 
-    bias = bias_table[:, bias_index()].transpose(1, 0, 2).reshape(SPAN, heads * SPAN)
+    bias = pl.pallas_call(
+        bias_kernel,
+        out_shape=jax.ShapeDtypeStruct((SPAN, heads * SPAN), F32),
+        in_specs=[vmem],
+        out_specs=vmem,
+        compiler_params=params(),
+        cost_estimate=pl.CostEstimate(flops=1500000000, bytes_accessed=1000000, transcendentals=0),
+    )(jnp.tile(jnp.pad(bias_table, ((0, 0), (0, -bias_table.shape[1] % LANES))).T, (1, WIN)))
     scale = jnp.repeat(attn_scale, head)[None]
     gain_a, gain_m = gain_attn[None], gain_mlp[None]
     rolled = ahead(wave_tokens, 0)
@@ -330,7 +368,7 @@
             jax.ShapeDtypeStruct(wave_tokens.shape, BF16),
             wide, wide, wide, wide32, wide32,
             jax.ShapeDtypeStruct((tokens * width // LANES, LANES // head * SPAN), BF16),
-            wide, wide32, one, jax.ShapeDtypeStruct((tokens, hidden), F32), wide32, one,
+            wide, wide32, one, jax.ShapeDtypeStruct((tokens, hidden), BF16), wide32, one,
         ),
         in_specs=[vmem] * 9,
         out_specs=(vmem,) * 13,
@@ -351,6 +389,7 @@
         compiler_params=params(),
         cost_estimate=pl.CostEstimate(flops=10000000000, bytes_accessed=8000000, transcendentals=0),
     )(cot, w_qkv, w_proj, w_fc1, w_fc2, gain_a, gain_m, scale, *res[1:])
+    piece, grad = lax.optimization_barrier((piece, grad))
     row_grad = moved(grad[s:, :far], 1, 0)
     col_grad = moved(grad[: tok_rows - s, far:], 0, 1)
     cor_grad = moved(grad[s:, far:], 1, 1)

time: 118 us -> 87.2 us (0.74)
  local copies, waits for them, and re-layouts: 41.1 us -> 12.3 us
  Pallas kernels: 42.6 us -> 31.3 us
  waiting for transfers between devices: 8.2 us -> 18.1 us
    gather x2 -> x0, local copies, waits for them, and re-layouts: 16.4 us -> none  [local(): bias_table[:, bias_index()].transpose(1, 0, 2).reshape(SPAN, heads * SPAN)]
    unnamed x72 -> x35, local copies, waits for them, and re-layouts: 19.5 us -> 7.83 us
    ppermute x9, waiting for transfers between devices: 8.2 us -> 14.8 us  [moved(): return lax.ppermute(piece, ('gx', 'gy'), route)]
    pallas_call x1, Pallas kernels: 11.1 us -> 5.83 us  [local(): pl.pallas_call(forward_kernel, out_shape=(jax.ShapeDtypeStruct(wave_token...]
    pallas_call x1, Pallas kernels: 15.5 us -> 11.9 us  [local(): pl.pallas_call(lambda a, b, c, d, e, f: readout_kernel(ext_cols, a, b, c,...]
    pallas_call x1, Pallas kernels: 11 us -> 7.6 us  [local(): pl.pallas_call(backward_kernel, out_shape=jax.ShapeDtypeStruct(wave_token...]
    all_to_all x1, waiting for transfers between devices: 0.01 us -> 1.83 us  [local(): lax.all_to_all(send, ('gx', 'gy'), split_axis=0, concat_axis=0, tiled=True)]
    all_to_all x1, waiting for transfers between devices: 0.01 us -> 1.39 us  [local(): lax.all_to_all(mix, ('gx', 'gy'), split_axis=0, concat_axis=0, tiled=True)]
  transfers between devices with their start and end apart: 11 -> 11, of which waited for: 3 -> 3; matrix products, arithmetic and copies ran while one was open for 19% -> 6% of each run, Pallas kernels for 21% -> 20%
where the time goes in v1:
time: 87.2 us; the launch traced here: 86.6 us
  Pallas kernels  31.3 us (36%)
  starting transfers between devices  21.5 us (25%)
  waiting for transfers between devices  18.1 us (21%)
  local copies, waits for them, and re-layouts  12.3 us (14%)
  other arithmetic  1.76 us (2%)
  between operations  1.62 us (2%)
    ppermute x9, starting transfers between devices, moved(): return lax.ppermute(piece, ('gx', 'gy'), route)  16.1 us
    ppermute x9, waiting for transfers between devices, moved(): return lax.ppermute(piece, ('gx', 'gy'), route)  14.8 us
    pallas_call x1, Pallas kernels, local(): pl.pallas_call(lambda a, b, c, d, e, f: readout_kernel(ext_cols, a, b, c,...  11.9 us
    unnamed x35, local copies, waits for them, and re-layouts  7.83 us
    pallas_call x1, Pallas kernels, local(): pl.pallas_call(backward_kernel, out_shape=jax.ShapeDtypeStruct(wave_token...  7.6 us
    pallas_call x1, Pallas kernels, local(): pl.pallas_call(forward_kernel, out_shape=(jax.ShapeDtypeStruct(wave_token...  5.83 us
    pallas_call x1, Pallas kernels, local(): pl.pallas_call(lambda *refs: order_kernel(tok_rows, tok_cols, row_devs, c...  2.9 us
    all_to_all x1, starting transfers between devices, local(): lax.all_to_all(mix, ('gx', 'gy'), split_axis=0, concat_axis=0, tiled=True)  2.83 us
  transfers between devices with their start and end apart: 11, of which 3 were waited for; matrix products, arithmetic and copies ran while one was open for 6% of the time, Pallas kernels for 20%

profile of v1, /device:TPU:0, one launch (start us, length us, event | category | flops | bytes accessed | tf_op | source)
XLA Modules:
  0.0 86.6 jit_solution(11548873415497048558)
XLA Ops:
  0.6 1.2 %fusion.2 = (bf16[4,28,512]{2,1,0:T(8,128)(2,1)S(1)}, bf16[4,28,512]{2,1,0:T(8,128)(2,1)S(1)}, bf16[4,28,512]{2,1,0:T(8,128)(2,1)S(1)}, bf16[4,28,512]{2,1,0:T(8,128)(2,1)S(1)}) fusion(bf16[8,32,512]{2,1,0:T(8,128)(2,1)} %param.19, bf16[8,32,512]{2,1,0:T(8,128)(2,1)} %param.18), kind=kLoop, calls=%fused_computation.11 | loop fusion | bytes 917504 | tf_op jit(solution)/shard_map/slice | solution.py:333
  2.6 4.5 %collective-permute-start.1 = (bf16[8,28,512]{2,1,0:T(8,128)(2,1)}, bf16[8,28,512]{2,1,0:T(8,128)(2,1)}, u32[]{:S(2)}, u32[]{:S(2)}) collective-permute-start(bf16[8,28,512]{2,1,0:T(8,128)(2,1)} %pad_maximum_fusion), channel_id=1, source_target_pairs={{0,28},{1,29},{2,30},{3,31},{4,0},{5,1},{6,2},{7,3},{8,4},{9,5},{1... | collective-permute-start | bytes 688136 | tf_op jit(solution)/shard_map/ppermute | solution.py:306
  7.9 2.5 %collective-permute-start = (bf16[8,4,512]{2,1,0:T(4,128)(2,1)S(1)}, bf16[8,4,512]{2,1,0:T(4,128)(2,1)S(1)}, u32[]{:S(2)}, u32[]{:S(2)}) collective-permute-start(bf16[8,4,512]{2,1,0:T(4,128)(2,1)S(1)} %pad_maximum_fusion.1), channel_id=1, source_target_pairs={{0,3},{1,0},{2,1},{3,2},{4,7},{5,4},{6,5},{7,6},{8,11},{9,8},{10,9... | collective-permute-start | bytes 98312 | tf_op jit(solution)/shard_map/ppermute | solution.py:306
  11.6 1.1 %copy-done.6 = bf16[1,768,512]{2,1,0:T(8,128)(2,1)S(1)} copy-done((bf16[1,768,512]{2,1,0:T(8,128)(2,1)S(1)}, bf16[1,768,512]{2,1,0:T(8,128)(2,1)}, u32[]{:S(2)}) %copy-start.6) | copy-done | bytes 786456
  12.7 1.0 %copy-done.8 = bf16[512,512]{1,0:T(8,128)(2,1)S(1)} copy-done((bf16[512,512]{1,0:T(8,128)(2,1)S(1)}, bf16[512,512]{1,0:T(8,128)(2,1)}, u32[]{:S(2)}) %copy-start.8) | copy-done | bytes 524312
  14.5 2.9 %shard_map.195 = (bf16[768,640]{1,0:T(8,128)(2,1)}, s32[1,768]{1,0:T(1,128)S(1)}) custom-call(bf16[768,512]{1,0:T(8,128)(2,1)S(1)} %bitcast.17, s32[1,768]{1,0:T(1,128)S(1)} %copy-done.11, s32[3,768]{1,0:T(4,128)S(1)} %bitcast.16, bf16[512,512]{1,0:T(8,128)(2,1)S(1)} %copy-done.8), custom_call_target="tpu_custom_call" | custom-call | flops 3000000000 | bytes 3000000 | tf_op jit(solution)/shard_map/pallas_call | solution.py:337
  17.4 2.6 %all-to-all-start = ((bf16[32,24,640]{2,1,0:T(8,128)(2,1)}), bf16[32,24,640]{2,1,0:T(8,128)(2,1)S(1)}, u32[]{:S(2)}, u32[]{:S(2)}) async-start(bf16[32,24,640]{2,1,0:T(8,128)(2,1)} %bitcast.5), calls=%async_computation | async-start | bytes 1966080 | tf_op jit(solution)/shard_map/all_to_all | solution.py:348
  20.2 1.0 %shard_map.193.bias_ref = f32[64,1024]{1,0:T(8,128)S(1)} custom-call(f32[256,128]{1,0:T(8,128)S(1)} %copy.22.table_ref), custom_call_target="tpu_custom_call" | custom-call | flops 1500000000 | bytes 1000000 | tf_op jit(solution)/shard_map/pallas_call | solution.py:350
  21.6 1.0 %fusion.3 = (bf16[4,28,512]{2,1,0:T(8,128)(2,1)S(1)}, bf16[4,28,512]{2,1,0:T(8,128)(2,1)S(1)}) fusion(bf16[8,28,512]{2,1,0:T(8,128)(2,1)} %collective-permute-done.1), kind=kLoop, calls=%fused_computation.12 | loop fusion | bytes 458752 | tf_op jit(solution)/shard_map/slice | solution.py:334
  22.6 1.6 %copy-done = bf16[512,2048]{1,0:T(8,128)(2,1)S(1)} copy-done((bf16[512,2048]{1,0:T(8,128)(2,1)S(1)}, bf16[512,2048]{1,0:T(8,128)(2,1)}, u32[]{:S(2)}) %copy-start) | copy-done | bytes 2097176
  24.2 1.6 %copy-done.2 = bf16[2048,512]{1,0:T(8,128)(2,1)S(1)} copy-done((bf16[2048,512]{1,0:T(8,128)(2,1)S(1)}, bf16[2048,512]{1,0:T(8,128)(2,1)}, u32[]{:S(2)}) %copy-start.2) | copy-done | bytes 2097176
  25.8 1.0 %copy-done.9 = bf16[512,512]{1,0:T(8,128)(2,1)S(1)} copy-done((bf16[512,512]{1,0:T(8,128)(2,1)S(1)}, bf16[512,512]{1,0:T(8,128)(2,1)}, u32[]{:S(2)}) %copy-start.9) | copy-done | bytes 524312
  26.9 5.8 %shard_map.194 = (bf16[8,32,512]{2,1,0:T(8,128)(2,1)S(1)}, bf16[256,512]{1,0:T(8,128)(2,1)S(1)}, bf16[256,512]{1,0:T(8,128)(2,1)S(1)}, bf16[256,512]{1,0:T(8,128...) custom-call(bf16[8,32,512]{2,1,0:T(8,128)(2,1)S(1)} %maximum_maximum, ...), custom_call_target="tpu_custom_call" | custom-call | flops 8000000000 | bytes 8000000 | tf_op jit(solution)/shard_map/pallas_call | solution.py:365
  32.9 1.7 %collective-permute-start.5 = (bf16[5,4,512]{2,1,0:T(4,128)(2,1)S(1)}, bf16[5,4,512]{2,1,0:T(4,128)(2,1)S(1)}, u32[]{:S(2)}, u32[]{:S(2)}) collective-permute-start(bf16[5,4,512]{2,1,0:T(4,128)(2,1)S(1)} %slice.81), channel_id=1, source_target_pairs={{0,1},{1,2},{2,3},{3,0},{4,5},{5,6},{6,7},{7,4},{8,9},{9,10},{10,1... | collective-permute-start | bytes 61448 | tf_op jit(solution)/shard_map/ppermute | solution.py:306
  34.6 2.3 %collective-permute-start.3 = (bf16[4,4,512]{2,1,0:T(4,128)(2,1)S(1)}, bf16[4,4,512]{2,1,0:T(4,128)(2,1)S(1)}, u32[]{:S(2)}, u32[]{:S(2)}) collective-permute-start(bf16[4,4,512]{2,1,0:T(4,128)(2,1)S(1)} %slice.79), channel_id=1, source_target_pairs={{0,5},{1,6},{2,7},{3,4},{4,9},{5,10},{6,11},{7,8},{8,13},{9,14},{1... | collective-permute-start | bytes 49160 | tf_op jit(solution)/shard_map/ppermute | solution.py:306
  37.0 7.6 %shard_map.196 = bf16[8,32,512]{2,1,0:T(8,128)(2,1)S(1)} custom-call(bf16[8,32,512]{2,1,0:T(8,128)(2,1)S(1)} %maximum_maximum_fusion.2.cot_ref, bf16[512,1536]{1,0:T(8,128)(2,1)S(1)} %copy-done.4, bf16[512,512]{1,0:T(8,128)(2,1)S(1)} %copy-done.9, bf16[512,2048]{1,0:T(8,128)(2,1)S(1)} %copy-done.1, bf16[2048,512]{1,0:T(8,128)(2,1)S(1)} %copy-done.3, ...), custom_call_target="tpu_custom_call" | custom-call | flops 10000000000 | bytes 8000000 | tf_op jit(solution)/shard_map/pallas_call | solution.py:383
  44.9 1.8 %all-to-all-done = bf16[32,24,640]{2,1,0:T(8,128)(2,1)S(1)} async-done(((bf16[32,24,640]{2,1,0:T(8,128)(2,1)}), bf16[32,24,640]{2,1,0:T(8,128)(2,1)S(1)}, u32[]{:S(2)}, u32[]{:S(2)}) %all-to-all-start) | async-done | bytes 983072 | tf_op jit(solution)/shard_map/all_to_all | solution.py:348
  46.7 11.9 %shard_map.197 = bf16[768,512]{1,0:T(8,128)(2,1)} custom-call(bf16[768,640]{1,0:T(8,128)(2,1)S(1)} %bitcast.14, bf16[384,512]{1,0:T(8,128)(2,1)S(1)} %pad.9.b, bf16[512,1024]{1,0:T(8,128)(2,1)S(1)} %copy-done.5, f32[1,512]{1,0:T(1,128)S(1)} %broadcast_in_dim_reshape.7.d), custom_call_target="tpu_custom_call" | custom-call | flops 8000000000 | bytes 3000000 | tf_op jit(solution)/shard_map/pallas_call | solution.py:411
  58.7 2.8 %all-to-all-start.1 = ((bf16[32,24,512]{2,1,0:T(8,128)(2,1)}), bf16[32,24,512]{2,1,0:T(8,128)(2,1)S(1)}, u32[]{:S(2)}, u32[]{:S(2)}) async-start(bf16[32,24,512]{2,1,0:T(8,128)(2,1)} %bitcast.7), calls=%async_computation.1 | async-start | bytes 1572864 | tf_op jit(solution)/shard_map/all_to_all | solution.py:424
  61.9 2.8 %collective-permute-start.6 = (bf16[4,4,512]{2,1,0:T(4,128)(2,1)S(1)}, bf16[4,4,512]{2,1,0:T(4,128)(2,1)S(1)}, u32[]{:S(2)}, u32[]{:S(2)}) collective-permute-start(bf16[4,4,512]{2,1,0:T(4,128)(2,1)S(1)} %get-tuple-element.37), channel_id=1, source_target_pairs={{0,5},{1,6},{2,7},{3,4},{4,9},{5,10},{6,11},{7,8},{8,13},{9,14},{1... | collective-permute-start | bytes 49160 | tf_op jit(solution)/shard_map/ppermute | solution.py:306
  64.6 1.5 %collective-permute-start.8 = (bf16[4,4,512]{2,1,0:T(4,128)(2,1)S(1)}, bf16[4,4,512]{2,1,0:T(4,128)(2,1)S(1)}, u32[]{:S(2)}, u32[]{:S(2)}) collective-permute-start(bf16[4,4,512]{2,1,0:T(4,128)(2,1)S(1)} %get-tuple-element.38), channel_id=1, source_target_pairs={{0,1},{1,2},{2,3},{3,0},{4,5},{5,6},{6,7},{7,4},{8,9},{9,10},{10,1... | collective-permute-start | bytes 49160 | tf_op jit(solution)/shard_map/ppermute | solution.py:306
  67.5 14.8 %collective-permute-done.6 = bf16[4,4,512]{2,1,0:T(4,128)(2,1)S(1)} collective-permute-done((bf16[4,4,512]{2,1,0:T(4,128)(2,1)S(1)}, bf16[4,4,512]{2,1,0:T(4,128)(2,1)S(1)}, u32[]{:S(2)}, u32[]{:S(2)}) %collective-permute-start.6) | collective-permute-done | bytes 16416 | tf_op jit(solution)/shard_map/ppermute | solution.py:306
  83.1 1.4 %all-to-all-done.1 = bf16[32,24,512]{2,1,0:T(8,128)(2,1)S(1)} async-done(((bf16[32,24,512]{2,1,0:T(8,128)(2,1)}), bf16[32,24,512]{2,1,0:T(8,128)(2,1)S(1)}, u32[]{:S(2)}, u32[]{:S(2)}) %all-to-all-start.1) | async-done | bytes 786464 | tf_op jit(solution)/shard_map/all_to_all | solution.py:424
  84.5 2.1 %shard_map.198 = bf16[768,512]{1,0:T(8,128)(2,1)} custom-call(bf16[768,512]{1,0:T(8,128)(2,1)S(1)} %bitcast.15, s32[1,768]{1,0:T(1,128)S(1)} %get-tuple-element.36.pos_ref, bf16[768,512]{1,0:T(8,128)(2,1)S(1)} %bitcast.18, bf16[512,512]{1,0:T(8,128)(2,1)S(1)} %copy-done.10, s32[1]{0:T(128)S(6)} %copy.26.live_ref), custom_call_target="tpu_custom_call" | custom-call | flops 1500000000 | bytes 3000000 | tf_op jit(solution)/shard_map/pallas_call | solution.py:425
  (67 shorter events, 6.3 us)
Async XLA Ops:
  2.6 19.0 %collective-permute-start.1 = (bf16[8,28,512]{2,1,0:T(8,128)(2,1)}, bf16[8,28,512]{2,1,0:T(8,128)(2,1)}, u32[]{:S(2)}, u32[]{:S(2)}) collective-permute-start(bf16[8,28,512]{2,1,0:T(8,128)(2,1)} %pad_maximum_fusion), channel_id=1, source_target_pairs={{0,28},{1,29},{2,30},{3,31},{4,0},{5,1},{6,2},{7,3},{8,4},{9,5},{1... | collective-permute-start | bytes 688136 | tf_op jit(solution)/shard_map/ppermute | solution.py:306
  7.9 13.5 %collective-permute-start = (bf16[8,4,512]{2,1,0:T(4,128)(2,1)S(1)}, bf16[8,4,512]{2,1,0:T(4,128)(2,1)S(1)}, u32[]{:S(2)}, u32[]{:S(2)}) collective-permute-start(bf16[8,4,512]{2,1,0:T(4,128)(2,1)S(1)} %pad_maximum_fusion.1), channel_id=1, source_target_pairs={{0,3},{1,0},{2,1},{3,2},{4,7},{5,4},{6,5},{7,6},{8,11},{9,8},{10,9... | collective-permute-start | bytes 98312 | tf_op jit(solution)/shard_map/ppermute | solution.py:306
  10.5 11.0 %collective-permute-start.2 = (bf16[8,4,512]{2,1,0:T(4,128)(2,1)S(1)}, bf16[8,4,512]{2,1,0:T(4,128)(2,1)S(1)}, u32[]{:S(2)}, u32[]{:S(2)}) collective-permute-start(bf16[8,4,512]{2,1,0:T(4,128)(2,1)S(1)} %pad_maximum_fusion.2), channel_id=1, source_target_pairs={{0,31},{1,28},{2,29},{3,30},{4,3},{5,0},{6,1},{7,2},{8,7},{9,4},{1... | collective-permute-start | bytes 98312 | tf_op jit(solution)/shard_map/ppermute | solution.py:306
  11.6 1.1 %copy-start.6 = (bf16[1,768,512]{2,1,0:T(8,128)(2,1)S(1)}, bf16[1,768,512]{2,1,0:T(8,128)(2,1)}, u32[]{:S(2)}) copy-start(bf16[1,768,512]{2,1,0:T(8,128)(2,1)} %param.32) | copy-start | bytes 2359300
  14.5 5.5 %copy-start.14 = (f32[16,225]{1,0:T(8,128)S(1)}, f32[16,225]{1,0:T(8,128)}, u32[]{:S(2)}) copy-start(f32[16,225]{1,0:T(8,128)} %param.27) | copy-start | bytes 43204
  17.4 29.4 %all-to-all-start = ((bf16[32,24,640]{2,1,0:T(8,128)(2,1)}), bf16[32,24,640]{2,1,0:T(8,128)(2,1)S(1)}, u32[]{:S(2)}, u32[]{:S(2)}) async-start(bf16[32,24,640]{2,1,0:T(8,128)(2,1)} %bitcast.5), calls=%async_computation | async-start | bytes 1966080 | tf_op jit(solution)/shard_map/all_to_all | solution.py:348
  20.2 1.2 %copy-start.16 = (f32[16]{0:T(128)S(1)}, f32[16]{0:T(128)}, u32[]{:S(2)}) copy-start(f32[16]{0:T(128)} %param.31) | copy-start | bytes 196
  20.2 2.4 %copy-start.4 = (bf16[512,1536]{1,0:T(8,128)(2,1)S(1)}, bf16[512,1536]{1,0:T(8,128)(2,1)}, u32[]{:S(2)}) copy-start(bf16[512,1536]{1,0:T(8,128)(2,1)} %w_qkv.3) | copy-start | bytes 4718596
  20.2 2.4 %copy-start.12 = (f32[512]{0:T(512)S(1)}, f32[512]{0:T(512)}, u32[]{:S(2)}) copy-start(f32[512]{0:T(512)} %param.24) | copy-start | bytes 6148
  20.2 2.4 %copy-start.13 = (f32[512]{0:T(512)S(1)}, f32[512]{0:T(512)}, u32[]{:S(2)}) copy-start(f32[512]{0:T(512)} %param.25) | copy-start | bytes 6148
  22.6 1.6 %copy-start = (bf16[512,2048]{1,0:T(8,128)(2,1)S(1)}, bf16[512,2048]{1,0:T(8,128)(2,1)}, u32[]{:S(2)}) copy-start(bf16[512,2048]{1,0:T(8,128)(2,1)} %w_fc1.3) | copy-start | bytes 6291460
  24.2 1.6 %copy-start.2 = (bf16[2048,512]{1,0:T(8,128)(2,1)S(1)}, bf16[2048,512]{1,0:T(8,128)(2,1)}, u32[]{:S(2)}) copy-start(bf16[2048,512]{1,0:T(8,128)(2,1)} %w_fc2.3) | copy-start | bytes 6291460
  26.9 10.1 %copy-start.1 = (bf16[512,2048]{1,0:T(8,128)(2,1)S(1)}, bf16[512,2048]{1,0:T(8,128)(2,1)}, u32[]{:S(2)}) copy-start(bf16[512,2048]{1,0:T(8,128)(2,1)} %w_fc1.3) | copy-start | bytes 6291460
  26.9 10.1 %copy-start.3 = (bf16[2048,512]{1,0:T(8,128)(2,1)S(1)}, bf16[2048,512]{1,0:T(8,128)(2,1)}, u32[]{:S(2)}) copy-start(bf16[2048,512]{1,0:T(8,128)(2,1)} %w_fc2.3) | copy-start | bytes 6291460
  32.8 11.9 %collective-permute-start.4 = (bf16[4,29,512]{2,1,0:T(8,128)(2,1)S(1)}, bf16[4,29,512]{2,1,0:T(8,128)(2,1)S(1)}, u32[]{:S(2)}, u32[]{:S(2)}) collective-permute-start(bf16[4,29,512]{2,1,0:T(8,128)(2,1)S(1)} %slice.80), channel_id=1, source_target_pairs={{0,4},{1,5},{2,6},{3,7},{4,8},{5,9},{6,10},{7,11},{8,12},{9,13},{1... | collective-permute-start | bytes 356360 | tf_op jit(solution)/shard_map/ppermute | solution.py:306
  32.9 11.7 %collective-permute-start.5 = (bf16[5,4,512]{2,1,0:T(4,128)(2,1)S(1)}, bf16[5,4,512]{2,1,0:T(4,128)(2,1)S(1)}, u32[]{:S(2)}, u32[]{:S(2)}) collective-permute-start(bf16[5,4,512]{2,1,0:T(4,128)(2,1)S(1)} %slice.81), channel_id=1, source_target_pairs={{0,1},{1,2},{2,3},{3,0},{4,5},{5,6},{6,7},{7,4},{8,9},{9,10},{10,1... | collective-permute-start | bytes 61448 | tf_op jit(solution)/shard_map/ppermute | solution.py:306
  34.6 10.0 %collective-permute-start.3 = (bf16[4,4,512]{2,1,0:T(4,128)(2,1)S(1)}, bf16[4,4,512]{2,1,0:T(4,128)(2,1)S(1)}, u32[]{:S(2)}, u32[]{:S(2)}) collective-permute-start(bf16[4,4,512]{2,1,0:T(4,128)(2,1)S(1)} %slice.79), channel_id=1, source_target_pairs={{0,5},{1,6},{2,7},{3,4},{4,9},{5,10},{6,11},{7,8},{8,13},{9,14},{1... | collective-permute-start | bytes 49160 | tf_op jit(solution)/shard_map/ppermute | solution.py:306
  44.6 2.2 %copy-start.5 = (bf16[512,1024]{1,0:T(8,128)(2,1)S(1)}, bf16[512,1024]{1,0:T(8,128)(2,1)}, u32[]{:S(2)}) copy-start(bf16[512,1024]{1,0:T(8,128)(2,1)} %c.1) | copy-start | bytes 3145732
  58.7 25.8 %copy-start.7 = (bf16[1,768,512]{2,1,0:T(8,128)(2,1)S(1)}, bf16[1,768,512]{2,1,0:T(8,128)(2,1)}, u32[]{:S(2)}) copy-start(bf16[1,768,512]{2,1,0:T(8,128)(2,1)} %param.32) | copy-start | bytes 2359300
  58.7 25.8 %copy-start.10 = (bf16[512,512]{1,0:T(8,128)(2,1)S(1)}, bf16[512,512]{1,0:T(8,128)(2,1)}, u32[]{:S(2)}) copy-start(bf16[512,512]{1,0:T(8,128)(2,1)} %w_ref.1) | copy-start | bytes 1572868
  58.7 25.8 %all-to-all-start.1 = ((bf16[32,24,512]{2,1,0:T(8,128)(2,1)}), bf16[32,24,512]{2,1,0:T(8,128)(2,1)S(1)}, u32[]{:S(2)}, u32[]{:S(2)}) async-start(bf16[32,24,512]{2,1,0:T(8,128)(2,1)} %bitcast.7), calls=%async_computation.1 | async-start | bytes 1572864 | tf_op jit(solution)/shard_map/all_to_all | solution.py:424
  61.5 20.8 %collective-permute-start.7 = (bf16[4,28,512]{2,1,0:T(8,128)(2,1)S(1)}, bf16[4,28,512]{2,1,0:T(8,128)(2,1)S(1)}, u32[]{:S(2)}, u32[]{:S(2)}) collective-permute-start(bf16[4,28,512]{2,1,0:T(8,128)(2,1)S(1)} %get-tuple-element.39), channel_id=1, source_target_pairs={{0,4},{1,5},{2,6},{3,7},{4,8},{5,9},{6,10},{7,11},{8,12},{9,13},{1... | collective-permute-start | bytes 344072 | tf_op jit(solution)/shard_map/ppermute | solution.py:306
  61.9 20.4 %collective-permute-start.6 = (bf16[4,4,512]{2,1,0:T(4,128)(2,1)S(1)}, bf16[4,4,512]{2,1,0:T(4,128)(2,1)S(1)}, u32[]{:S(2)}, u32[]{:S(2)}) collective-permute-start(bf16[4,4,512]{2,1,0:T(4,128)(2,1)S(1)} %get-tuple-element.37), channel_id=1, source_target_pairs={{0,5},{1,6},{2,7},{3,4},{4,9},{5,10},{6,11},{7,8},{8,13},{9,14},{1... | collective-permute-start | bytes 49160 | tf_op jit(solution)/shard_map/ppermute | solution.py:306
  64.6 17.7 %collective-permute-start.8 = (bf16[4,4,512]{2,1,0:T(4,128)(2,1)S(1)}, bf16[4,4,512]{2,1,0:T(4,128)(2,1)S(1)}, u32[]{:S(2)}, u32[]{:S(2)}) collective-permute-start(bf16[4,4,512]{2,1,0:T(4,128)(2,1)S(1)} %get-tuple-element.38), channel_id=1, source_target_pairs={{0,1},{1,2},{2,3},{3,0},{4,5},{5,6},{6,7},{7,4},{8,9},{9,10},{10,1... | collective-permute-start | bytes 49160 | tf_op jit(solution)/shard_map/ppermute | solution.py:306
  (4 other events, 3.8 us)

commit v2 on v1

--- a/solution.py
+++ b/solution.py
@@ -61,8 +61,19 @@
 
 def forward_kernel(
     x_ref, w_qkv, w_proj, w_fc1, w_fc2, gain_attn, gain_mlp, scale_ref, bias_ref,
-    out_ref, qs_ref, kn_ref, v_ref, rq_ref, rk_ref, p_ref, mixed_ref, u1_ref, i1_ref, dg_ref, u2_ref, i2_ref,
+    out_ref, *rest,
 ):
+    kept, (proj_buf, fc1_buf, fc2_buf), held, (sems, kept_sems) = rest[:12], rest[12:15], rest[15:27], rest[27:]
+    qs_ref, kn_ref, v_ref, rq_ref, rk_ref, p_ref, mixed_ref, u1_ref, i1_ref, dg_ref, u2_ref, i2_ref = held
+    stores = [
+        pltpu.make_async_copy(src, dst, kept_sems.at[i]) for i, (src, dst) in enumerate(zip(held, kept))
+    ]
+    loads = [
+        pltpu.make_async_copy(src, dst, sems.at[i])
+        for i, (src, dst) in enumerate(((w_proj, proj_buf), (w_fc1, fc1_buf), (w_fc2, fc2_buf)))
+    ]
+    for load in loads:
+        load.start()
     width = x_ref.shape[-1]
     head = width // (bias_ref.shape[1] // SPAN)
     per = LANES // head
@@ -102,25 +113,36 @@
             rows = slice(w * SPAN, (w + 1) * SPAN)
             vb = jnp.concatenate([v[rows]] * per, 0) * mask
             mixed_ref[rows, at] = dot(p[rows], vb).astype(BF16)
-    u1, i1 = norm_parts(dot(mixed_ref[...], w_proj[...]))
+    for store in stores[:7]:
+        store.start()
+    loads[0].wait()
+    u1, i1 = norm_parts(dot(mixed_ref[...], proj_buf[...]))
     u1_ref[...] = u1
-    i1_ref[...] = i1
+    i1_ref[...] = jnp.broadcast_to(i1, i1_ref.shape)
+    for store in stores[7:9]:
+        store.start()
     h1 = (x + u1 * gain_attn[...]).astype(BF16)
     mlp = jnp.zeros(x.shape, F32)
     step = width
+    loads[1].wait()
+    loads[2].wait()
     for c in range(w_fc1.shape[1] // step):
         cols = slice(c * step, (c + 1) * step)
-        z = dot(h1, w_fc1[:, cols])
+        z = dot(h1, fc1_buf[:, cols])
         zz = z * z
         t = jnp.tanh(GELU_A * z * (1.0 + GELU_B * zz))
         half = 0.5 * (1.0 + t)
         slope = GELU_A + 3.0 * GELU_A * GELU_B * zz
         dg_ref[:, cols] = (half + 0.5 * z * (1.0 - t * t) * slope).astype(BF16)
-        mlp = mlp + dot((z * half).astype(BF16), w_fc2[cols, :])
+        mlp = mlp + dot((z * half).astype(BF16), fc2_buf[cols, :])
     u2, i2 = norm_parts(mlp)
     u2_ref[...] = u2
-    i2_ref[...] = i2
+    i2_ref[...] = jnp.broadcast_to(i2, i2_ref.shape)
+    for store in stores[9:]:
+        store.start()
     out_ref[...] = from_windows(h1.astype(F32) + u2 * gain_mlp[...]).astype(BF16)
+    for store in stores:
+        store.wait()
 
 
 def unit_back(cot, unit, inv, sum_ones):
@@ -130,16 +152,33 @@
 
 
 def backward_kernel(
-    cot_ref, w_qkv, w_proj, w_fc1, w_fc2, gain_attn, gain_mlp, scale_ref,
-    qs_ref, kn_ref, v_ref, rq_ref, rk_ref, p_ref, mixed_ref, u1_ref, i1_ref, dg_ref, u2_ref, i2_ref,
-    grad_ref, dm_ref,
+    cot_ref, qkv_hbm, proj_hbm, fc1_hbm, fc2_hbm, gain_attn, gain_mlp, scale_ref, *rest
 ):
+    kept, (grad_ref, dm_ref), (w_proj, w_fc1, w_fc2, w_qkv), held, (sems,) = (
+        rest[:12], rest[12:14], rest[14:18], rest[18:30], rest[30:]
+    )
+    qs_ref, kn_ref, v_ref, rq_ref, rk_ref, p_ref, mixed_ref, u1_ref, i1_ref, dg_ref, u2_ref, i2_ref = held
+    pairs = list(zip(kept, held)) + [
+        (proj_hbm, w_proj), (fc1_hbm, w_fc1), (fc2_hbm, w_fc2), (qkv_hbm, w_qkv)
+    ]
+    loads = [pltpu.make_async_copy(src, dst, sems.at[i]) for i, (src, dst) in enumerate(pairs)]
+    stages = ((10, 11), (14, 9, 13), (7, 8, 12), (0, 1, 2, 3, 4, 5, 6, 15))
+    for stage in stages:
+        for i in stage:
+            loads[i].start()
+
+    def arrive(stage):
+        for i in stages[stage]:
+            loads[i].wait()
+
     width = cot_ref.shape[-1]
     per = p_ref.shape[1] // SPAN
     head = LANES // per
     cot = to_windows(cot_ref[...].astype(F32))
     windows = cot.shape[0] // SPAN
-    dmlp = norm_back(cot * gain_mlp[...], u2_ref[...], i2_ref[...]).astype(BF16)
+    arrive(0)
+    dmlp = norm_back(cot * gain_mlp[...], u2_ref[...], i2_ref[:, :1]).astype(BF16)
+    arrive(1)
     dh = jnp.zeros(cot.shape, F32)
     step = width
     for c in range(w_fc1.shape[1] // step):
@@ -147,13 +186,15 @@
         dz = dot(dmlp, w_fc2[cols, :], NT) * dg_ref[:, cols].astype(F32)
         dh = dh + dot(dz.astype(BF16), w_fc1[:, cols], NT)
     dh = (cot + dh).astype(BF16).astype(F32)
-    dproj = norm_back(dh * gain_attn[...], u1_ref[...], i1_ref[...]).astype(BF16)
+    arrive(2)
+    dproj = norm_back(dh * gain_attn[...], u1_ref[...], i1_ref[:, :1]).astype(BF16)
     dm_ref[...] = dot(dproj, w_proj[...], NT).astype(BF16)
     sum_ones = block_ones(LANES, LANES, head, head)
     sum_ones = jnp.concatenate([sum_ones, sum_ones], 0)
     mask = block_ones(per * SPAN, LANES, SPAN, head)
     mask32 = mask.astype(F32)
     dx = dh
+    arrive(3)
     for g in range(width // LANES):
         at = slice(g * LANES, (g + 1) * LANES)
         dm = dm_ref[:, at]
@@ -187,8 +228,14 @@
     grad_ref[...] = from_windows(dx).astype(BF16)
 
 
-def order_kernel(tok_rows, tok_cols, row_devs, col_devs, feat_ref, patch_ref, cover_ref, w_ref, send_ref, pos_ref):
+def order_kernel(tok_rows, tok_cols, row_devs, col_devs, feat_ref, patch_ref, cover_ref, w_ref, send_ref, pos_ref, feat_buf, w_buf, sems):
     slots, width = feat_ref.shape
+    loads = [
+        pltpu.make_async_copy(feat_ref, feat_buf, sems.at[0]),
+        pltpu.make_async_copy(w_ref, w_buf, sems.at[1]),
+    ]
+    for load in loads:
+        load.start()
     devs = row_devs * col_devs
     grid_cols = tok_cols * col_devs
     patch = patch_ref[...]
@@ -204,7 +251,9 @@
     pos = target * (slots // devs) + rank
     pos_ref[...] = pos
     place = jnp.where(i == pos, 1.0, 0.0).astype(BF16)
-    query = dot(feat_ref[...], w_ref[...]).astype(BF16)
+    for load in loads:
+        load.wait()
+    query = dot(feat_buf[...], w_buf[...]).astype(BF16)
     send_ref[:, :width] = dot(place, query).astype(BF16)
     which = lax.broadcasted_iota(jnp.int32, (LANES, slots), 0)
     meta = jnp.where(which == 0, (row % tok_rows).astype(F32), 0.0)
@@ -323,6 +372,7 @@
     feat = floe_feat[0]
     slots = feat.shape[0]
     vmem = pl.BlockSpec(memory_space=pltpu.VMEM)
+    anywhere = pl.BlockSpec(memory_space=pltpu.HBM)
     s = SHIFT
 
     row_in = moved(jnp.concatenate([wave_tokens[:s, s:], grad_out[:s, s:]], 0), -1, 0)
@@ -340,9 +390,14 @@
             jax.ShapeDtypeStruct((slots, width + LANES), BF16),
             jax.ShapeDtypeStruct((1, slots), jnp.int32),
         ),
-        in_specs=[vmem] * 4,
+        in_specs=[anywhere, vmem, vmem, anywhere],
         out_specs=(vmem, vmem),
-        compiler_params=params(),
+        scratch_shapes=[
+            pltpu.VMEM(feat.shape, BF16),
+            pltpu.VMEM(r_wq.shape, BF16),
+            pltpu.SemaphoreType.DMA((2,)),
+        ],
+        compiler_params=params(58),
         cost_estimate=pl.CostEstimate(flops=3000000000, bytes_accessed=3000000, transcendentals=0),
     )(feat, floe_patch, floe_cover[0], r_wq)
     piece = lax.all_to_all(send, ("gx", "gy"), split_axis=0, concat_axis=0, tiled=True)
@@ -361,18 +416,21 @@
     cot = ahead(grad_out, 1)
     wide = jax.ShapeDtypeStruct((tokens, width), BF16)
     wide32 = jax.ShapeDtypeStruct((tokens, width), F32)
-    one = jax.ShapeDtypeStruct((tokens, 1), F32)
+    one = jax.ShapeDtypeStruct((tokens, LANES), F32)
+    kept = (
+        wide, wide, wide, wide32, wide32,
+        jax.ShapeDtypeStruct((tokens * width // LANES, LANES // head * SPAN), BF16),
+        wide, wide32, one, jax.ShapeDtypeStruct((tokens, hidden), BF16), wide32, one,
+    )
+    held = [pltpu.VMEM(k.shape, k.dtype) for k in kept]
+    weights = [pltpu.VMEM(w.shape, BF16) for w in (w_proj, w_fc1, w_fc2)]
     res = pl.pallas_call(
         forward_kernel,
-        out_shape=(
-            jax.ShapeDtypeStruct(wave_tokens.shape, BF16),
-            wide, wide, wide, wide32, wide32,
-            jax.ShapeDtypeStruct((tokens * width // LANES, LANES // head * SPAN), BF16),
-            wide, wide32, one, jax.ShapeDtypeStruct((tokens, hidden), BF16), wide32, one,
-        ),
-        in_specs=[vmem] * 9,
-        out_specs=(vmem,) * 13,
-        compiler_params=params(),
+        out_shape=(jax.ShapeDtypeStruct(wave_tokens.shape, BF16),) + kept,
+        in_specs=[vmem, vmem, anywhere, anywhere, anywhere] + [vmem] * 4,
+        out_specs=(vmem,) + (anywhere,) * 12,
+        scratch_shapes=weights + held + [pltpu.SemaphoreType.DMA((3,)), pltpu.SemaphoreType.DMA((12,))],
+        compiler_params=params(58),
         cost_estimate=pl.CostEstimate(flops=8000000000, bytes_accessed=8000000, transcendentals=1000000),
     )(rolled, w_qkv, w_proj, w_fc1, w_fc2, gain_a, gain_m, scale, bias)
     out = res[0]
@@ -380,20 +438,6 @@
     row_out = moved(out[s:, : far + 1], 1, 0)
     col_out = moved(out[:near, far:], 0, 1)
     cor_out = moved(out[s:, far:], 1, 1)
-    grad = pl.pallas_call(
-        backward_kernel,
-        out_shape=jax.ShapeDtypeStruct(wave_tokens.shape, BF16),
-        in_specs=[vmem] * 20,
-        out_specs=vmem,
-        scratch_shapes=[pltpu.VMEM((tokens, width), BF16)],
-        compiler_params=params(),
-        cost_estimate=pl.CostEstimate(flops=10000000000, bytes_accessed=8000000, transcendentals=0),
-    )(cot, w_qkv, w_proj, w_fc1, w_fc2, gain_a, gain_m, scale, *res[1:])
-    piece, grad = lax.optimization_barrier((piece, grad))
-    row_grad = moved(grad[s:, :far], 1, 0)
-    col_grad = moved(grad[: tok_rows - s, far:], 0, 1)
-    cor_grad = moved(grad[s:, far:], 1, 1)
-
     ext = jnp.concatenate(
         [
             jnp.concatenate([cor_out, row_out], 1),
@@ -421,7 +465,25 @@
         compiler_params=params(),
         cost_estimate=pl.CostEstimate(flops=8000000000, bytes_accessed=3000000, transcendentals=1000000),
     )(piece, table, r_wkv, jnp.repeat(read_scale, head)[None])
+    mix, cot = lax.optimization_barrier((mix, cot))
     back = lax.all_to_all(mix, ("gx", "gy"), split_axis=0, concat_axis=0, tiled=True)
+    grad = pl.pallas_call(
+        backward_kernel,
+        out_shape=jax.ShapeDtypeStruct(wave_tokens.shape, BF16),
+        in_specs=[vmem] + [anywhere] * 4 + [vmem] * 3 + [anywhere] * 12,
+        out_specs=vmem,
+        scratch_shapes=[pltpu.VMEM((tokens, width), BF16)]
+        + weights
+        + [pltpu.VMEM(w_qkv.shape, BF16)]
+        + held
+        + [pltpu.SemaphoreType.DMA((16,))],
+        compiler_params=params(58),
+        cost_estimate=pl.CostEstimate(flops=10000000000, bytes_accessed=8000000, transcendentals=0),
+    )(cot, w_qkv, w_proj, w_fc1, w_fc2, gain_a, gain_m, scale, *res[1:])
+    row_grad = moved(grad[s:, :far], 1, 0)
+    col_grad = moved(grad[: tok_rows - s, far:], 0, 1)
+    cor_grad = moved(grad[s:, far:], 1, 1)
+
     floe_out = pl.pallas_call(
         finish_kernel,
         out_shape=jax.ShapeDtypeStruct((slots, width), BF16),

time: 87.2 us -> 87.1 us (level)
  waiting for transfers between devices: 18.1 us -> 5.68 us
  Pallas kernels: 31.3 us -> 43.7 us
  local copies, waits for them, and re-layouts: 12.3 us -> 11.3 us
    ppermute x9, waiting for transfers between devices: 14.8 us -> 5.57 us  [moved(): return lax.ppermute(piece, ('gx', 'gy'), route)]
    pallas_call x1, Pallas kernels: 5.83 us -> 11.7 us  [local(): pl.pallas_call(forward_kernel, out_shape=(jax.ShapeDtypeStruct(wave_token...]
    unnamed x35 -> x17, local copies, waits for them, and re-layouts: 7.83 us -> 2.04 us
    pallas_call x1, Pallas kernels: 7.6 us -> 12.2 us  [local(): pl.pallas_call(backward_kernel, out_shape=jax.ShapeDtypeStruct(wave_token...]
    pallas_call x1, Pallas kernels: 2.9 us -> 4.73 us  [local(): pl.pallas_call(lambda *refs: order_kernel(tok_rows, tok_cols, row_devs, c...]
    all_to_all x1, waiting for transfers between devices: 1.83 us -> 0.01 us  [local(): lax.all_to_all(send, ('gx', 'gy'), split_axis=0, concat_axis=0, tiled=True)]
    concatenate x2, other arithmetic: 0.09 us -> 1.48 us  [ahead(): return jnp.concatenate([upper, lower], 0)]
    all_to_all x1, waiting for transfers between devices: 1.39 us -> 0.1 us  [local(): lax.all_to_all(mix, ('gx', 'gy'), split_axis=0, concat_axis=0, tiled=True)]
  transfers between devices with their start and end apart: 11 -> 11, of which waited for: 3 -> 4; matrix products, arithmetic and copies ran while one was open for 6% -> 14% of each run, Pallas kernels for 20% -> 34%
where the time goes in v2:
time: 87.1 us; the launch traced here: 86.4 us
  Pallas kernels  43.7 us (50%)
  starting transfers between devices  21.8 us (25%)
  local copies, waits for them, and re-layouts  11.3 us (13%)
  waiting for transfers between devices  5.68 us (7%)
  other arithmetic  2.46 us (3%)
  between operations  1.55 us (2%)
    ppermute x9, starting transfers between devices, moved(): return lax.ppermute(piece, ('gx', 'gy'), route)  16.1 us
    pallas_call x1, Pallas kernels, local(): pl.pallas_call(backward_kernel, out_shape=jax.ShapeDtypeStruct(wave_token...  12.2 us
    pallas_call x1, Pallas kernels, local(): pl.pallas_call(lambda a, b, c, d, e, f: readout_kernel(ext_cols, a, b, c,...  11.9 us
    pallas_call x1, Pallas kernels, local(): pl.pallas_call(forward_kernel, out_shape=(jax.ShapeDtypeStruct(wave_token...  11.7 us
    ppermute x9, waiting for transfers between devices, moved(): return lax.ppermute(piece, ('gx', 'gy'), route)  5.57 us
    pallas_call x1, Pallas kernels, local(): pl.pallas_call(lambda *refs: order_kernel(tok_rows, tok_cols, row_devs, c...  4.73 us
    all_to_all x1, starting transfers between devices, local(): lax.all_to_all(mix, ('gx', 'gy'), split_axis=0, concat_axis=0, tiled=True)  2.95 us
    all_to_all x1, starting transfers between devices, local(): lax.all_to_all(send, ('gx', 'gy'), split_axis=0, concat_axis=0, tiled=True)  2.66 us
  transfers between devices with their start and end apart: 11, of which 4 were waited for; matrix products, arithmetic and copies ran while one was open for 14% of the time, Pallas kernels for 34%

profile of v2, /device:TPU:0, one launch (start us, length us, event | category | flops | bytes accessed | tf_op | source)
XLA Modules:
  0.0 86.4 jit_solution(14736704481581303188)
XLA Ops:
  0.6 0.8 fusion.5
  1.5 6.4 %collective-permute-start.2 = (bf16[8,4,512]{2,1,0:T(4,128)(2,1)S(1)}, bf16[8,4,512]{2,1,0:T(4,128)(2,1)S(1)}, u32[]{:S(2)}, u32[]{:S(2)}) collective-permute-start(bf16[8,4,512]{2,1,0:T(4,128)(2,1)S(1)} %pad_maximum_fusion.2), channel_id=1, source_target_pairs={{0,31},{1,28},{2,29},{3,30},{4,3},{5,0},{6,1},{7,2},{8,7},{9,4},{1... | collective-permute-start | bytes 98312 | tf_op jit(solution)/shard_map/ppermute | solution.py:355
  8.5 1.2 %fusion.2 = (bf16[4,28,512]{2,1,0:T(8,128)(2,1)S(1)}, bf16[4,28,512]{2,1,0:T(8,128)(2,1)S(1)}, bf16[4,28,512]{2,1,0:T(8,128)(2,1)S(1)}, bf16[4,28,512]{2,1,0:T(8,128)(2,1)S(1)}) fusion(bf16[8,32,512]{2,1,0:T(8,128)(2,1)} %param.19, bf16[8,32,512]{2,1,0:T(8,128)(2,1)} %param.18), kind=kLoop, calls=%fused_computation.11 | loop fusion | bytes 917504 | tf_op jit(solution)/shard_map/slice | solution.py:383
  10.4 1.3 %copy.25 = s32[1,3,768]{2,1,0:T(4,128)} copy(s32[1,3,768]{2,0,1:T(1,128)} %param.35) | data formatting | bytes 18432
  11.7 4.7 %shard_map.195 = (bf16[768,640]{1,0:T(8,128)(2,1)}, s32[1,768]{1,0:T(1,128)}) custom-call(bf16[768,512]{1,0:T(8,128)(2,1)} %bitcast.16, s32[1,768]{1,0:T(1,128)} %refs_1_.1, s32[3,768]{1,0:T(4,128)} %bitcast.20, bf16[512,512]{1,0:T(8,128)(2,1)} %refs_3_.1), custom_call_target="tpu_custom_call" | custom-call | flops 3000000000 | bytes 3000000 | tf_op jit(solution)/shard_map/pallas_call | solution.py:387
  16.5 2.7 %all-to-all-start = ((bf16[32,24,640]{2,1,0:T(8,128)(2,1)}), bf16[32,24,640]{2,1,0:T(8,128)(2,1)S(1)}, u32[]{:S(2)}, u32[]{:S(2)}) async-start(bf16[32,24,640]{2,1,0:T(8,128)(2,1)} %bitcast.18), calls=%async_computation | async-start | bytes 1966080 | tf_op jit(solution)/shard_map/all_to_all | solution.py:403
  19.3 1.0 %shard_map.193.bias_ref = f32[64,1024]{1,0:T(8,128)S(1)} custom-call(f32[256,128]{1,0:T(8,128)S(1)} %copy.22.table_ref), custom_call_target="tpu_custom_call" | custom-call | flops 1500000000 | bytes 1000000 | tf_op jit(solution)/shard_map/pallas_call | solution.py:405
  22.7 11.7 %shard_map.194 = (bf16[8,32,512]{2,1,0:T(8,128)(2,1)}, bf16[256,512]{1,0:T(8,128)(2,1)}, bf16[256,512]{1,0:T(8,128)(2,1)}, bf16[256,512]{1,0:T(8,128)(2,1)}, f32...) custom-call(bf16[8,32,512]{2,1,0:T(8,128)(2,1)} %maximum_maximum_fus, ...), custom_call_target="tpu_custom_call" | custom-call | flops 8000000000 | bytes 8000000 | tf_op jit(solution)/shard_map/pallas_call | solution.py:427
  34.5 0.9 slice.79
  36.1 0.9 %slice.80 = bf16[4,29,512]{2,1,0:T(8,128)(2,1)S(1)} slice(bf16[8,32,512]{2,1,0:T(8,128)(2,1)} %get-tuple-element.20), slice={[4:8], [0:29], [0:512]} | slice | bytes 237568 | tf_op jit(solution)/shard_map/slice | solution.py:438
  37.0 1.5 %collective-permute-start.3 = (bf16[4,4,512]{2,1,0:T(4,128)(2,1)S(1)}, bf16[4,4,512]{2,1,0:T(4,128)(2,1)S(1)}, u32[]{:S(2)}, u32[]{:S(2)}) collective-permute-start(bf16[4,4,512]{2,1,0:T(4,128)(2,1)S(1)} %slice.79), channel_id=1, source_target_pairs={{0,5},{1,6},{2,7},{3,4},{4,9},{5,10},{6,11},{7,8},{8,13},{9,14},{1... | collective-permute-start | bytes 49160 | tf_op jit(solution)/shard_map/ppermute | solution.py:355
  38.5 1.5 %collective-permute-start.5 = (bf16[5,4,512]{2,1,0:T(4,128)(2,1)S(1)}, bf16[5,4,512]{2,1,0:T(4,128)(2,1)S(1)}, u32[]{:S(2)}, u32[]{:S(2)}) collective-permute-start(bf16[5,4,512]{2,1,0:T(4,128)(2,1)S(1)} %slice.81), channel_id=1, source_target_pairs={{0,1},{1,2},{2,3},{3,0},{4,5},{5,6},{6,7},{7,4},{8,9},{9,10},{10,1... | collective-permute-start | bytes 61448 | tf_op jit(solution)/shard_map/ppermute | solution.py:355
  40.0 1.1 %collective-permute-start.4 = (bf16[4,29,512]{2,1,0:T(8,128)(2,1)S(1)}, bf16[4,29,512]{2,1,0:T(8,128)(2,1)S(1)}, u32[]{:S(2)}, u32[]{:S(2)}) collective-permute-start(bf16[4,29,512]{2,1,0:T(8,128)(2,1)S(1)} %slice.80), channel_id=1, source_target_pairs={{0,4},{1,5},{2,6},{3,7},{4,8},{5,9},{6,10},{7,11},{8,12},{9,13},{1... | collective-permute-start | bytes 356360 | tf_op jit(solution)/shard_map/ppermute | solution.py:355
  41.8 0.9 %slice.82 = bf16[5,29,512]{2,1,0:T(8,128)(2,1)S(1)} slice(bf16[8,32,512]{2,1,0:T(8,128)(2,1)} %get-tuple-element.20), slice={[0:5], [0:29], [0:512]} | slice | bytes 296960 | tf_op jit(solution)/shard_map/slice | solution.py:444
  42.7 1.4 %collective-permute-done.3 = bf16[4,4,512]{2,1,0:T(4,128)(2,1)S(1)} collective-permute-done((bf16[4,4,512]{2,1,0:T(4,128)(2,1)S(1)}, bf16[4,4,512]{2,1,0:T(4,128)(2,1)S(1)}, u32[]{:S(2)}, u32[]{:S(2)}) %collective-permute-start.3) | collective-permute-done | bytes 16416 | tf_op jit(solution)/shard_map/ppermute | solution.py:355
  44.1 2.1 %collective-permute-done.4 = bf16[4,29,512]{2,1,0:T(8,128)(2,1)S(1)} collective-permute-done((bf16[4,29,512]{2,1,0:T(8,128)(2,1)S(1)}, bf16[4,29,512]{2,1,0:T(8,128)(2,1)S(1)}, u32[]{:S(2)}, u32[]{:S(2)}) %collective-permute-start.4) | collective-permute-done | bytes 118816 | tf_op jit(solution)/shard_map/ppermute | solution.py:355
  46.4 11.9 %shard_map.196 = bf16[768,512]{1,0:T(8,128)(2,1)} custom-call(bf16[768,640]{1,0:T(8,128)(2,1)S(1)} %bitcast.14, bf16[384,512]{1,0:T(8,128)(2,1)S(1)} %pad.9.b, bf16[512,1024]{1,0:T(8,128)(2,1)S(1)} %copy-done, f32[1,512]{1,0:T(1,128)S(1)} %broadcast_in_dim_reshape.7.d), custom_call_target="tpu_custom_call" | custom-call | flops 8000000000 | bytes 3000000 | tf_op jit(solution)/shard_map/pallas_call | solution.py:455
  58.4 2.9 %all-to-all-start.1 = ((bf16[32,24,512]{2,1,0:T(8,128)(2,1)}), bf16[32,24,512]{2,1,0:T(8,128)(2,1)S(1)}, u32[]{:S(2)}, u32[]{:S(2)}) async-start(bf16[32,24,512]{2,1,0:T(8,128)(2,1)} %bitcast.7), calls=%async_computation.1 | async-start | bytes 1572864 | tf_op jit(solution)/shard_map/all_to_all | solution.py:469
  61.4 12.2 %shard_map.197 = bf16[8,32,512]{2,1,0:T(8,128)(2,1)} custom-call(bf16[8,32,512]{2,1,0:T(8,128)(2,1)} %maximum_maximum_fusion.2.cot_ref, bf16[512,1536]{1,0:T(8,128)(2,1)} %qkv_hbm.1, bf16[512,512]{1,0:T(8,128)(2,1)} %proj_hbm.1, bf16[512,2048]{1,0:T(8,128)(2,1)} %fc1_hbm.1, bf16[2048,512]{1,0:T(8,128)(2,1)} %fc2_hbm.1, f32[1,512]{1,0:T(1,128)} %bitcast.22, ...), custom_call_target="tpu_custom_call" | custom-call | flops 10000000000 | bytes 8000000 | tf_op jit(solution)/shard_map/pallas_call | solution.py:470
  73.6 1.0 %fusion.1 = (bf16[4,28,512]{2,1,0:T(8,128)(2,1)S(1)}, bf16[4,28,512]{2,1,0:T(8,128)(2,1)S(1)}) fusion(bf16[8,32,512]{2,1,0:T(8,128)(2,1)} %shard_map.197), kind=kLoop, calls=%fused_computation.10 | loop fusion | bytes 458752 | tf_op jit(solution)/shard_map/slice | solution.py:483
  75.7 2.8 %collective-permute-start.6 = (bf16[4,4,512]{2,1,0:T(4,128)(2,1)S(1)}, bf16[4,4,512]{2,1,0:T(4,128)(2,1)S(1)}, u32[]{:S(2)}, u32[]{:S(2)}) collective-permute-start(bf16[4,4,512]{2,1,0:T(4,128)(2,1)S(1)} %get-tuple-element.37), channel_id=1, source_target_pairs={{0,5},{1,6},{2,7},{3,4},{4,9},{5,10},{6,11},{7,8},{8,13},{9,14},{1... | collective-permute-start | bytes 49160 | tf_op jit(solution)/shard_map/ppermute | solution.py:355
  78.4 1.5 %collective-permute-start.8 = (bf16[4,4,512]{2,1,0:T(4,128)(2,1)S(1)}, bf16[4,4,512]{2,1,0:T(4,128)(2,1)S(1)}, u32[]{:S(2)}, u32[]{:S(2)}) collective-permute-start(bf16[4,4,512]{2,1,0:T(4,128)(2,1)S(1)} %get-tuple-element.38), channel_id=1, source_target_pairs={{0,1},{1,2},{2,3},{3,0},{4,5},{5,6},{6,7},{7,4},{8,9},{9,10},{10,1... | collective-permute-start | bytes 49160 | tf_op jit(solution)/shard_map/ppermute | solution.py:355
  81.3 2.1 %collective-permute-done.6 = bf16[4,4,512]{2,1,0:T(4,128)(2,1)S(1)} collective-permute-done((bf16[4,4,512]{2,1,0:T(4,128)(2,1)S(1)}, bf16[4,4,512]{2,1,0:T(4,128)(2,1)S(1)}, u32[]{:S(2)}, u32[]{:S(2)}) %collective-permute-start.6) | collective-permute-done | bytes 16416 | tf_op jit(solution)/shard_map/ppermute | solution.py:355
  84.3 2.1 %shard_map.198 = bf16[768,512]{1,0:T(8,128)(2,1)} custom-call(bf16[768,512]{1,0:T(8,128)(2,1)S(1)} %bitcast.15, s32[1,768]{1,0:T(1,128)S(1)} %copy-done.4, bf16[768,512]{1,0:T(8,128)(2,1)S(1)} %bitcast.17, bf16[512,512]{1,0:T(8,128)(2,1)S(1)} %copy-done.2, s32[1]{0:T(128)S(6)} %copy.26.live_ref), custom_call_target="tpu_custom_call" | custom-call | flops 1500000000 | bytes 3000000 | tf_op jit(solution)/shard_map/pallas_call | solution.py:487
  (49 shorter events, 8.3 us)
Async XLA Ops:
  1.5 20.4 %collective-permute-start.2 = (bf16[8,4,512]{2,1,0:T(4,128)(2,1)S(1)}, bf16[8,4,512]{2,1,0:T(4,128)(2,1)S(1)}, u32[]{:S(2)}, u32[]{:S(2)}) collective-permute-start(bf16[8,4,512]{2,1,0:T(4,128)(2,1)S(1)} %pad_maximum_fusion.2), channel_id=1, source_target_pairs={{0,31},{1,28},{2,29},{3,30},{4,3},{5,0},{6,1},{7,2},{8,7},{9,4},{1... | collective-permute-start | bytes 98312 | tf_op jit(solution)/shard_map/ppermute | solution.py:355
  8.0 13.9 %collective-permute-start = (bf16[8,4,512]{2,1,0:T(4,128)(2,1)S(1)}, bf16[8,4,512]{2,1,0:T(4,128)(2,1)S(1)}, u32[]{:S(2)}, u32[]{:S(2)}) collective-permute-start(bf16[8,4,512]{2,1,0:T(4,128)(2,1)S(1)} %pad_maximum_fusion.1), channel_id=1, source_target_pairs={{0,3},{1,0},{2,1},{3,2},{4,7},{5,4},{6,5},{7,6},{8,11},{9,8},{10,9... | collective-permute-start | bytes 98312 | tf_op jit(solution)/shard_map/ppermute | solution.py:355
  9.8 12.1 %collective-permute-start.1 = (bf16[8,28,512]{2,1,0:T(8,128)(2,1)S(1)}, bf16[8,28,512]{2,1,0:T(8,128)(2,1)S(1)}, u32[]{:S(2)}, u32[]{:S(2)}) collective-permute-start(bf16[8,28,512]{2,1,0:T(8,128)(2,1)S(1)} %pad_maximum_fusion), channel_id=1, source_target_pairs={{0,28},{1,29},{2,30},{3,31},{4,0},{5,1},{6,2},{7,3},{8,4},{9,5},{1... | collective-permute-start | bytes 688136 | tf_op jit(solution)/shard_map/ppermute | solution.py:355
  11.7 7.4 %copy-start.5 = (f32[16,225]{1,0:T(8,128)S(1)}, f32[16,225]{1,0:T(8,128)}, u32[]{:S(2)}) copy-start(f32[16,225]{1,0:T(8,128)} %param.27) | copy-start | bytes 43204
  16.5 29.9 %all-to-all-start = ((bf16[32,24,640]{2,1,0:T(8,128)(2,1)}), bf16[32,24,640]{2,1,0:T(8,128)(2,1)S(1)}, u32[]{:S(2)}, u32[]{:S(2)}) async-start(bf16[32,24,640]{2,1,0:T(8,128)(2,1)} %bitcast.18), calls=%async_computation | async-start | bytes 1966080 | tf_op jit(solution)/shard_map/all_to_all | solution.py:403
  19.3 1.7 %copy-start.6 = (f32[16]{0:T(128)S(1)}, f32[16]{0:T(128)}, u32[]{:S(2)}) copy-start(f32[16]{0:T(128)} %param.26) | copy-start | bytes 196
  19.3 2.4 %copy-start.7 = (f32[16]{0:T(128)S(1)}, f32[16]{0:T(128)}, u32[]{:S(2)}) copy-start(f32[16]{0:T(128)} %param.31) | copy-start | bytes 196
  20.3 0.7 copy-start.3
  34.4 12.0 %copy-start = (bf16[512,1024]{1,0:T(8,128)(2,1)S(1)}, bf16[512,1024]{1,0:T(8,128)(2,1)}, u32[]{:S(2)}) copy-start(bf16[512,1024]{1,0:T(8,128)(2,1)} %c.1) | copy-start | bytes 3145732
  37.0 7.0 %collective-permute-start.3 = (bf16[4,4,512]{2,1,0:T(4,128)(2,1)S(1)}, bf16[4,4,512]{2,1,0:T(4,128)(2,1)S(1)}, u32[]{:S(2)}, u32[]{:S(2)}) collective-permute-start(bf16[4,4,512]{2,1,0:T(4,128)(2,1)S(1)} %slice.79), channel_id=1, source_target_pairs={{0,5},{1,6},{2,7},{3,4},{4,9},{5,10},{6,11},{7,8},{8,13},{9,14},{1... | collective-permute-start | bytes 49160 | tf_op jit(solution)/shard_map/ppermute | solution.py:355
  38.5 5.6 %collective-permute-start.5 = (bf16[5,4,512]{2,1,0:T(4,128)(2,1)S(1)}, bf16[5,4,512]{2,1,0:T(4,128)(2,1)S(1)}, u32[]{:S(2)}, u32[]{:S(2)}) collective-permute-start(bf16[5,4,512]{2,1,0:T(4,128)(2,1)S(1)} %slice.81), channel_id=1, source_target_pairs={{0,1},{1,2},{2,3},{3,0},{4,5},{5,6},{6,7},{7,4},{8,9},{9,10},{10,1... | collective-permute-start | bytes 61448 | tf_op jit(solution)/shard_map/ppermute | solution.py:355
  40.0 6.2 %collective-permute-start.4 = (bf16[4,29,512]{2,1,0:T(8,128)(2,1)S(1)}, bf16[4,29,512]{2,1,0:T(8,128)(2,1)S(1)}, u32[]{:S(2)}, u32[]{:S(2)}) collective-permute-start(bf16[4,29,512]{2,1,0:T(8,128)(2,1)S(1)} %slice.80), channel_id=1, source_target_pairs={{0,4},{1,5},{2,6},{3,7},{4,8},{5,9},{6,10},{7,11},{8,12},{9,13},{1... | collective-permute-start | bytes 356360 | tf_op jit(solution)/shard_map/ppermute | solution.py:355
  58.4 25.9 %all-to-all-start.1 = ((bf16[32,24,512]{2,1,0:T(8,128)(2,1)}), bf16[32,24,512]{2,1,0:T(8,128)(2,1)S(1)}, u32[]{:S(2)}, u32[]{:S(2)}) async-start(bf16[32,24,512]{2,1,0:T(8,128)(2,1)} %bitcast.7), calls=%async_computation.1 | async-start | bytes 1572864 | tf_op jit(solution)/shard_map/all_to_all | solution.py:469
  61.3 23.0 %copy-start.1 = (bf16[1,768,512]{2,1,0:T(8,128)(2,1)S(1)}, bf16[1,768,512]{2,1,0:T(8,128)(2,1)}, u32[]{:S(2)}) copy-start(bf16[1,768,512]{2,1,0:T(8,128)(2,1)} %param.32) | copy-start | bytes 2359300
  61.3 23.0 %copy-start.2 = (bf16[512,512]{1,0:T(8,128)(2,1)S(1)}, bf16[512,512]{1,0:T(8,128)(2,1)}, u32[]{:S(2)}) copy-start(bf16[512,512]{1,0:T(8,128)(2,1)} %w_ref.1) | copy-start | bytes 1572868
  61.3 22.9 %copy-start.4 = (s32[1,768]{1,0:T(1,128)S(1)}, s32[1,768]{1,0:T(1,128)}, u32[]{:S(2)}) copy-start(s32[1,768]{1,0:T(1,128)} %get-tuple-element.36.pos_ref) | copy-start | bytes 9220
  74.6 8.8 %collective-permute-start.7 = (bf16[4,28,512]{2,1,0:T(8,128)(2,1)S(1)}, bf16[4,28,512]{2,1,0:T(8,128)(2,1)S(1)}, u32[]{:S(2)}, u32[]{:S(2)}) collective-permute-start(bf16[4,28,512]{2,1,0:T(8,128)(2,1)S(1)} %get-tuple-element.39), channel_id=1, source_target_pairs={{0,4},{1,5},{2,6},{3,7},{4,8},{5,9},{6,10},{7,11},{8,12},{9,13},{1... | collective-permute-start | bytes 344072 | tf_op jit(solution)/shard_map/ppermute | solution.py:355
  75.7 7.7 %collective-permute-start.6 = (bf16[4,4,512]{2,1,0:T(4,128)(2,1)S(1)}, bf16[4,4,512]{2,1,0:T(4,128)(2,1)S(1)}, u32[]{:S(2)}, u32[]{:S(2)}) collective-permute-start(bf16[4,4,512]{2,1,0:T(4,128)(2,1)S(1)} %get-tuple-element.37), channel_id=1, source_target_pairs={{0,5},{1,6},{2,7},{3,4},{4,9},{5,10},{6,11},{7,8},{8,13},{9,14},{1... | collective-permute-start | bytes 49160 | tf_op jit(solution)/shard_map/ppermute | solution.py:355
  78.4 5.0 %collective-permute-start.8 = (bf16[4,4,512]{2,1,0:T(4,128)(2,1)S(1)}, bf16[4,4,512]{2,1,0:T(4,128)(2,1)S(1)}, u32[]{:S(2)}, u32[]{:S(2)}) collective-permute-start(bf16[4,4,512]{2,1,0:T(4,128)(2,1)S(1)} %get-tuple-element.38), channel_id=1, source_target_pairs={{0,1},{1,2},{2,3},{3,0},{4,5},{5,6},{6,7},{7,4},{8,9},{9,10},{10,1... | collective-permute-start | bytes 49160 | tf_op jit(solution)/shard_map/ppermute | solution.py:355
